TPU v7x, 32 devices: a whole 2x2x4 slice. The times are simulated.
32 devices in a mesh: batch: 16 (over z, y, x), mp: 2 (over core).
Axes of the slice: x: 2, y: 2, z: 4, core: 2. Of those that a mesh axis runs over, the one named last changes fastest.
Arguments:
- hidden_in: bfloat16 [32, 1024, 768], P('batch', 'mp'), may hold values from -6 to 6
- memory_flags: int32 [32], P('batch'), may hold values 0 or 1
- memory_coeffs: bfloat16 [32, 256, 768], P('batch', 'mp'), may hold values from -6 to 6
- first_gain: float32 [768], replicated, may hold values from 0.25 to 1.75
- first_bias: float32 [768], replicated, may hold values from -1.5 to 1.5
- query_key_value_matrix: bfloat16 [768, 3, 768], P(None, None, 'mp'), may hold values from -0.21875 to 0.21875
- qv_bias: bfloat16 [2, 768], P(None, 'mp'), may hold values from -1.5 to 1.5
- memory_weight: bfloat16 [2, 12, 256], P(None, 'mp'), may hold values from -0.1875 to 0.1875
- memory_bias: bfloat16 [2, 12], P(None, 'mp'), may hold values from -1.5 to 1.5
- output_matrix: bfloat16 [768, 768], P('mp'), may hold values from -1.25 to 1.25
- out_bias: float32 [768], replicated, may hold values from -1.5 to 1.5
- second_gain: float32 [768], replicated, may hold values from 0.25 to 1.75
- second_bias: float32 [768], replicated, may hold values from -1.5 to 1.5
- up_matrix: bfloat16 [768, 3072], P(None, 'mp'), may hold values from -0.21875 to 0.21875
- up_bias_vector: bfloat16 [3072], P('mp'), may hold values from -1.5 to 1.5
- down_matrix: bfloat16 [3072, 768], P('mp'), may hold values from -0.109375 to 0.109375
- down_bias: float32 [768], replicated, may hold values from -1.5 to 1.5
- out_grad: bfloat16 [32, 1024, 768], P('batch', 'mp'), may hold values from -6 to 6
Outputs:
- block_out: bfloat16 [32, 1024, 768], P('batch', 'mp')
- input_grad: float32 [32, 1024, 768], P('batch', 'mp')
- coeff_grad: float32 [32, 256, 768], P('batch', 'mp')
- first_gain_grad: float32 [768], replicated
- first_bias_grad: float32 [768], replicated
- query_key_value_matrix_grad: float32 [768, 3, 768], P(None, None, 'mp')
- qv_bias_grad: float32 [2, 768], P(None, 'mp')
- memory_weight_grad: float32 [2, 12, 256], P(None, 'mp')
- memory_bias_grad: float32 [2, 12], P(None, 'mp')
- output_matrix_grad: float32 [768, 768], P('mp')
- out_bias_grad: float32 [768], replicated
- second_gain_grad: float32 [768], replicated
- second_bias_grad: float32 [768], replicated
- up_weight_grad: float32 [768, 3072], P(None, 'mp')
- up_bias_grad: float32 [3072], P('mp')
- down_weight_grad: float32 [3072, 768], P('mp')
- down_bias_grad: float32 [768], replicated
Inputs may be any that keep to these rules, and one draw needn't show every extreme that they name: memory_flags holds one flag per sequence.
All inputs are finite; a program needn't handle non-finite values. No bound on the sum of `memory_flags` on one device may be relied on, other than what follows from the above.
Results may differ from a plain program's by a relative error of at most 0.013.
The roundings to bfloat16 on the way count: a program that leaves them out, or rounds other values in their place, can miss the bound.
Values may be sent and summed in bfloat16 or wider, within the bound.
No kernel may reach another device: no remote copies, remote signals or barrier semaphores. Data moves between devices by JAX's collectives and lax.ppermute only.
A program may use at most 320 MiB of HBM per device.

v0:
```python
import functools
import math

import jax
import jax.numpy as jnp
from jax import lax
from jax.experimental import pallas as pl
from jax.experimental.pallas import tpu as pltpu
from jax.sharding import PartitionSpec as P

HD = 64
BLOCK = 256
FEED_BLOCK = 512
BF16 = jnp.bfloat16
F32 = jnp.float32
VMEM_BYTES = 56 * 2**20


def dot_nn(left, right):
    return lax.dot_general(left, right, (((1,), (0,)), ((), ())), preferred_element_type=F32)


def dot_nt(left, right):
    return lax.dot_general(left, right, (((1,), (1,)), ((), ())), preferred_element_type=F32)


def dot_tn(left, right):
    return lax.dot_general(left, right, (((0,), (0,)), ((), ())), preferred_element_type=F32)


def dot_tn_exact(left, right):
    return lax.dot_general(
        left,
        right,
        (((0,), (0,)), ((), ())),
        precision=lax.Precision.HIGHEST,
        preferred_element_type=F32,
    )


def three_parts(values):
    high = values.astype(BF16).astype(F32)
    rest = values - high
    middle = rest.astype(BF16).astype(F32)
    return jnp.concatenate([high, middle, rest - middle], axis=0).astype(BF16)


def add_parts(stacked):
    rows = stacked.shape[0] // 3
    return stacked[:rows] + stacked[rows : 2 * rows] + stacked[2 * rows :]


def scaled_rows(values):
    row_mean = jnp.mean(values, axis=-1, keepdims=True)
    centred = values - row_mean
    row_var = jnp.mean(centred * centred, axis=-1, keepdims=True)
    inverse = lax.rsqrt(row_var + 1e-05)
    return centred * inverse, inverse


def norm_back(grad_out, scaled, inverse, gain_vec):
    grad_scaled = grad_out * gain_vec
    first_mean = jnp.mean(grad_scaled, axis=-1, keepdims=True)
    second_mean = jnp.mean(grad_scaled * scaled, axis=-1, keepdims=True)
    return inverse * (grad_scaled - first_mean - scaled * second_mean)


def whole(shape):
    return pl.BlockSpec(shape, lambda *_: (0,) * len(shape))


class Order:
    def __init__(self):
        self.token = None

    def call(
        self, kernel, grid, in_specs, out_specs, out_shape, flops, name, operands, scratch=(), scalars=(),
        aliases=None,
    ):
        count = len(operands)
        prefetched = len(scalars)
        token = () if self.token is None else (self.token,)

        def body(*refs):
            kernel(*refs[: prefetched + count], *refs[prefetched + count + len(token) :])

        bytes_accessed = sum(math.prod(s.shape) * jnp.dtype(s.dtype).itemsize for s in out_shape)
        results = pl.pallas_call(
            body,
            grid_spec=pltpu.PrefetchScalarGridSpec(
                num_scalar_prefetch=prefetched,
                grid=grid,
                in_specs=list(in_specs) + [pl.BlockSpec(memory_space=pl.ANY)] * len(token),
                out_specs=list(out_specs),
                scratch_shapes=list(scratch),
            ),
            out_shape=out_shape,
            input_output_aliases=aliases or {},
            compiler_params=pltpu.CompilerParams(
                vmem_limit_bytes=VMEM_BYTES, dimension_semantics=("arbitrary",) * len(grid)
            ),
            cost_estimate=pl.CostEstimate(
                flops=int(flops), bytes_accessed=2 * bytes_accessed, transcendentals=0
            ),
            name=name,
        )(*scalars, *operands, *token)
        self.token = results[-1]
        return results


def shape_of(shape, dtype):
    return jax.ShapeDtypeStruct(shape, dtype)


def project_kernel(
    scalars, mine, theirs, vectors, w_own, w_far, qb, coeffs_mine, coeffs_theirs,
    hid, norm_t, q, k, v, mem_k, mem_v, coeffs_t,
):
    me = scalars[0]
    index = pl.program_id(0)

    @pl.when(index == me)
    def _():
        hid[...] = mine[0]

    @pl.when(index != me)
    def _():
        hid[...] = theirs[...]

    scaled, _ = scaled_rows(hid[...].astype(F32))
    normed = (scaled * vectors[0:1] + vectors[1:2]).astype(BF16)
    norm_t[...] = normed.T

    def weight(part):
        return jnp.concatenate([w_own[part], w_far[part]], axis=1)

    q[...] = (dot_nn(normed, weight(0)) + qb[0:1]).astype(BF16)
    k[...] = dot_nn(normed, weight(1)).astype(BF16)
    v[...] = (dot_nn(normed, weight(2)) + qb[1:2]).astype(BF16)

    @pl.when(index == 0)
    def _():
        first = coeffs_mine[0].astype(F32)
        second = coeffs_theirs[...].astype(F32)
        rows = jnp.concatenate(
            [jnp.where(me == 0, first, second), jnp.where(me == 0, second, first)], axis=0
        ).astype(BF16)
        coeffs_t[...] = rows.T
        mem_k[...] = dot_nn(rows, weight(1)).astype(BF16)
        mem_v[...] = dot_nn(rows, weight(2)).astype(BF16)


def project(order, scalars, hidden_in, hidden_come, vectors, w_own, w_far, qb, coeffs, coeffs_come):
    tokens, width = hidden_come.shape
    length = 2 * tokens
    part = coeffs_come.shape[0]
    basis = 2 * part
    rows = pl.BlockSpec((tokens, width), lambda i, s: (i, 0))
    return order.call(
        project_kernel,
        (2,),
        [
            pl.BlockSpec((1, tokens, width), lambda i, s: (s[0], 0, 0)),
            whole((tokens, width)),
            whole(vectors.shape),
            whole(w_own.shape),
            whole(w_far.shape),
            whole(qb.shape),
            pl.BlockSpec((1, part, width), lambda i, s: (s[0], 0, 0)),
            whole((part, width)),
        ],
        [
            rows,
            pl.BlockSpec((width, tokens), lambda i, s: (0, i)),
            rows,
            rows,
            rows,
            whole((basis, width)),
            whole((basis, width)),
            whole((width, basis)),
        ],
        [
            shape_of((length, width), BF16),
            shape_of((width, length), BF16),
            shape_of((length, width), BF16),
            shape_of((length, width), BF16),
            shape_of((length, width), BF16),
            shape_of((basis, width), BF16),
            shape_of((basis, width), BF16),
            shape_of((width, basis), BF16),
        ],
        2 * length * width * width * 3,
        "project",
        (hidden_in, hidden_come, vectors, w_own, w_far, qb, coeffs, coeffs_come),
        scalars=(scalars,),
    )


def head_rows(values_t, head):
    part = values_t[head * HD : (head + 1) * HD]
    zeros = jnp.zeros_like(part)
    return jnp.concatenate([part, zeros] if head == 0 else [zeros, part], axis=0)


def map_rows(mw, pair):
    return jnp.concatenate(
        [mw[2 * pair], mw[2 * pair + 1], jnp.zeros((4, mw.shape[2]), F32)], axis=0
    )


def pair_maps(rows, mem_k):
    maps = dot_nn(rows.astype(BF16), mem_k)
    row = lax.broadcasted_iota(jnp.int32, maps.shape, 0)
    lane = lax.broadcasted_iota(jnp.int32, maps.shape, 1)
    return jnp.where((row // 2) == (lane // HD), maps, 0.0)


def bias_rows(mb, pair):
    row = lax.broadcasted_iota(jnp.int32, (8, 1), 0)
    column = jnp.zeros((8, 1), F32)
    for head in range(2):
        for which in range(2):
            column = jnp.where(row == 2 * head + which, mb[which, 2 * pair + head], column)
    return column


def basis_of(logits, basis_count):
    centre = jax.nn.sigmoid(logits)
    softplus = jnp.maximum(logits, 0.0) + jnp.log(1.0 + jnp.exp(-jnp.abs(logits)))
    spread = 0.05 * softplus + (8.0 / basis_count) ** 2
    rate = -0.5 / spread
    level = lax.rsqrt(2.0 * math.pi * spread) / basis_count
    return centre, rate, level


def places_of(basis_count):
    steps = lax.broadcasted_iota(jnp.int32, (basis_count, BLOCK), 0).astype(F32)
    return (steps + 0.5) / basis_count


def attend_kernel(scalars, flags, q, k, v, mem_k, mem_v, mw, mb, att_t, mix_t, mix, stat):
    length = q.shape[0]
    basis = mem_k.shape[0]
    flag_value = flags[scalars[0]].astype(F32)
    q_t = (q[...].astype(F32) * 0.125).astype(BF16).T
    v_t = v[...].T
    mem_v_t = mem_v[...].T
    pair = pl.program_id(0)
    maps = pair_maps(map_rows(mw, pair), mem_k[...])
    logits = add_parts(dot_nn(three_parts(maps), q_t)) + bias_rows(mb, pair)
    centre, rate, level = basis_of(logits, basis)
    places = places_of(basis)
    allowed = lax.broadcasted_iota(jnp.int32, (BLOCK, BLOCK), 0) <= lax.broadcasted_iota(
        jnp.int32, (BLOCK, BLOCK), 1
    )
    stat[4:8, :] = logits[0:4]
    heads = []
    for head in range(2):
        rows = slice(head * HD, (head + 1) * HD)
        v_ones = jnp.concatenate([v_t[rows], jnp.ones((16, length), BF16)], axis=0)
        heads.append((rows, head_rows(q_t, head), v_ones))
    for index in range(length // BLOCK):
        start, stop = index * BLOCK, (index + 1) * BLOCK
        scores = []
        for rows, q_head, v_ones in heads:
            scores.append(dot_nn(k[:stop, :], q_head[:, start:stop]))
        for head, (rows, q_head, v_ones) in enumerate(heads):
            near = jnp.where(allowed, scores[head][start:], -1e30)
            top = jnp.max(near, axis=0, keepdims=True)
            if index:
                far = scores[head][:start]
                top = jnp.maximum(top, jnp.max(far, axis=0, keepdims=True))
                weights = jnp.concatenate([jnp.exp(far - top), jnp.exp(near - top)], axis=0)
            else:
                weights = jnp.exp(near - top)
            total = dot_nn(v_ones[:, :stop], weights.astype(BF16))
            denominator = total[HD : HD + 1]
            attended = total[:HD] / denominator
            att_t[rows, start:stop] = attended
            stat[head : head + 1, start:stop] = top + jnp.log(denominator)
            offset = places - centre[2 * head : 2 * head + 1, start:stop]
            mass = (
                jnp.exp(offset * offset * rate[2 * head + 1 : 2 * head + 2, start:stop])
                * level[2 * head + 1 : 2 * head + 2, start:stop]
            )
            recalled = dot_nn(mem_v_t[rows], mass.astype(BF16))
            mix_t[rows, start:stop] = (attended + flag_value * recalled).astype(BF16)
    mix[...] = mix_t[...].T


def attend(order, scalars, flags, q, k, v, mem_k, mem_v, mw, mb):
    length, width = q.shape
    basis = mem_k.shape[0]
    pairs = width // 128
    rows = pl.BlockSpec((length, 128), lambda p, *_: (0, p))
    mem_rows = pl.BlockSpec((basis, 128), lambda p, *_: (0, p))
    cols = pl.BlockSpec((128, length), lambda p, *_: (p, 0))
    return order.call(
        attend_kernel,
        (pairs,),
        [
            rows,
            rows,
            rows,
            mem_rows,
            mem_rows,
            whole(mw.shape),
            pl.BlockSpec(memory_space=pltpu.SMEM),
        ],
        [cols, cols, rows, pl.BlockSpec((8, length), lambda p, *_: (p, 0))],
        [
            shape_of((width, length), F32),
            shape_of((width, length), BF16),
            shape_of((length, width), BF16),
            shape_of((pairs * 8, length), F32),
        ],
        12 * length * length * width,
        "attend",
        (q, k, v, mem_k, mem_v, mw, mb),
        scalars=(scalars, flags),
    )


def attend_back_kernel(
    base, scalars, flags, q, k, v, mem_k, mem_v, mw, grad, att_t, stat, norm_t, coeffs_t, *refs
):
    dq, dk, dv, dmem_k, dmem_v, dqkv, dmw, sums = refs[-8:]
    length = q.shape[0]
    basis = mem_k.shape[0]
    flag_value = flags[scalars[0]].astype(F32)
    q_t = (q[...].astype(F32) * 0.125).astype(BF16).T
    k_t = k[...].T
    grad_t = grad[...].T
    lane = lax.broadcasted_iota(jnp.int32, (length, 128), 1)
    mem_rows = map_rows(mw, base + pl.program_id(0))
    maps = pair_maps(mem_rows, mem_k[...])
    logits = stat[4:8, :]
    logits = jnp.concatenate([logits, jnp.zeros_like(logits)], axis=0)
    centre, rate, level = basis_of(logits, basis)
    places = places_of(basis)
    allowed = lax.broadcasted_iota(jnp.int32, (BLOCK, BLOCK), 0) <= lax.broadcasted_iota(
        jnp.int32, (BLOCK, BLOCK), 1
    )
    q_lanes = []
    dk_lanes = []
    dv_lanes = []
    dmv_lanes = []
    mass_grads = []
    for head in range(2):
        rows = slice(head * HD, (head + 1) * HD)
        mine = (lane // HD) == head
        q_head_t = head_rows(q_t, head)
        grad_head_t = head_rows(grad_t, head)
        q_head = jnp.where(mine, q[...].astype(F32), 0.0).astype(BF16)
        grad_head = jnp.where(mine, grad[...].astype(F32), 0.0).astype(BF16)
        log_total = stat[head : head + 1, :]
        inner = jnp.sum(grad_t[rows].astype(F32) * att_t[rows], axis=0, keepdims=True)
        query_parts = [None] * (length // BLOCK)
        dk_parts = []
        dv_parts = []
        for index in range(length // BLOCK):
            start, stop = index * BLOCK, (index + 1) * BLOCK
            scores = dot_nn(k[start:stop, :], q_head_t[:, start:])
            weights = jnp.exp(scores - log_total[:, start:])
            diagonal = jnp.where(allowed, weights[:, :BLOCK], 0.0)
            if stop < length:
                weights = jnp.concatenate([diagonal, weights[:, BLOCK:]], axis=1)
            else:
                weights = diagonal
            weights_grad = dot_nn(v[start:stop, :], grad_head_t[:, start:])
            scores_grad = (weights * (weights_grad - inner[:, start:])).astype(BF16)
            dv_parts.append(dot_nn(weights.astype(BF16), grad_head[start:]))
            dk_parts.append(dot_nn(scores_grad, q_head[start:]))
            query = dot_nn(k_t[rows, start:stop], scores_grad)
            for later in range(index, length // BLOCK):
                piece = query[:, (later - index) * BLOCK : (later - index + 1) * BLOCK]
                kept = query_parts[later]
                query_parts[later] = piece if kept is None else kept + piece
        q_lanes.append(jnp.concatenate(query_parts, axis=1))
        dk_lanes.append(jnp.concatenate(dk_parts, axis=0))
        dv_lanes.append(jnp.concatenate(dv_parts, axis=0))
        sum_parts = []
        mem_total = None
        for index in range(length // BLOCK):
            start, stop = index * BLOCK, (index + 1) * BLOCK
            rate_row = rate[2 * head + 1 : 2 * head + 2, start:stop]
            offset = places - centre[2 * head : 2 * head + 1, start:stop]
            mass = (
                jnp.exp(offset * offset * rate_row) * level[2 * head + 1 : 2 * head + 2, start:stop]
            )
            basis_grad = dot_nn(mem_v[...], grad_head_t[:, start:stop])
            zeroth = basis_grad * mass
            first = zeroth * offset
            second = first * offset
            sum_parts.append(
                jnp.concatenate(
                    [
                        jnp.sum(first, axis=0, keepdims=True) * (-2.0 * rate_row),
                        jnp.sum(second, axis=0, keepdims=True) * (2.0 * rate_row * rate_row)
                        + jnp.sum(zeroth, axis=0, keepdims=True) * rate_row,
                    ],
                    axis=0,
                )
            )
            piece = dot_nn(mass.astype(BF16), grad_head[start:stop])
            mem_total = piece if mem_total is None else mem_total + piece
        dmv_lanes.append(mem_total)
        mass_grads.append(jnp.concatenate(sum_parts, axis=1))
    parity = lax.broadcasted_iota(jnp.int32, logits.shape, 0) % 2
    basis_grads = jnp.concatenate(
        mass_grads + [jnp.zeros((4, length), F32)], axis=0
    )
    slope = jnp.where(parity == 0, centre * (1.0 - centre), 0.05 * centre)
    logits_grad = basis_grads * slope * flag_value
    query_total = jnp.concatenate(q_lanes, axis=0) + dot_tn_exact(maps, logits_grad)
    dq[...] = (0.125 * query_total).T.astype(BF16)
    dk[...] = (0.125 * (dk_lanes[0] + dk_lanes[1])).astype(BF16)
    dv[...] = (dv_lanes[0] + dv_lanes[1]).astype(BF16)
    dmem_v[...] = (flag_value * (dmv_lanes[0] + dmv_lanes[1])).astype(BF16)
    row = lax.broadcasted_iota(jnp.int32, maps.shape, 0)
    lanes = lax.broadcasted_iota(jnp.int32, maps.shape, 1)
    outer = jnp.where(
        (row // 2) == (lanes // HD), add_parts(dot_nn(three_parts(logits_grad), q[...])) * 0.125, 0.0
    )
    dmem_k[...] = dot_tn_exact(mem_rows, outer).astype(BF16)
    dmw[0] = add_parts(dot_nt(three_parts(outer), mem_k[...]))
    ones = jnp.ones((16, length), BF16)
    sums[0, 0:8] = jnp.broadcast_to(jnp.sum(logits_grad, axis=1, keepdims=True), (8, 128))
    sums[0, 8:9] = dot_nn(ones, dq[...])[0:1]
    sums[0, 9:10] = dot_nn(ones, dv[...])[0:1]
    sums[0, 10:16] = jnp.zeros((6, 128), F32)
    width = norm_t.shape[0]
    rows_grad = dot_nn(norm_t[...], jnp.concatenate([dq[...], dk[...], dv[...]], axis=1))
    mem_grad = dot_nn(coeffs_t[...], jnp.concatenate([dmem_k[...], dmem_v[...]], axis=1))
    dqkv[:width] = rows_grad[:, :128].astype(BF16)
    dqkv[width : 2 * width] = (rows_grad[:, 128:256] + mem_grad[:, :128]).astype(BF16)
    dqkv[2 * width :] = (rows_grad[:, 256:] + mem_grad[:, 128:]).astype(BF16)


def attend_back(
    order, side, first, pairs, earlier, scalars, flags, q, k, v, mem_k, mem_v, mw, grad, att_t, stat, norm_t, coeffs_t
):
    length, width = q.shape
    basis = mem_k.shape[0]
    side_pairs = width // 256
    base = side * side_pairs + first
    half = width // 2
    rows = pl.BlockSpec((length, 128), lambda p, *_: (0, base + p))
    mem_rows = pl.BlockSpec((basis, 128), lambda p, *_: (0, base + p))
    out_rows = pl.BlockSpec((length, 128), lambda p, *_: (0, first + p))
    out_mem_rows = pl.BlockSpec((basis, 128), lambda p, *_: (0, first + p))
    operands = (q, k, v, mem_k, mem_v, mw, grad, att_t, stat, norm_t, coeffs_t)
    earlier = () if earlier is None else tuple(earlier)
    return order.call(
        functools.partial(attend_back_kernel, base),
        (pairs,),
        [
            rows,
            rows,
            rows,
            mem_rows,
            mem_rows,
            whole(mw.shape),
            rows,
            pl.BlockSpec((128, length), lambda p, *_: (base + p, 0)),
            pl.BlockSpec((8, length), lambda p, *_: (base + p, 0)),
            whole(norm_t.shape),
            whole(coeffs_t.shape),
        ]
        + [pl.BlockSpec(memory_space=pl.ANY)] * len(earlier),
        [
            out_rows,
            out_rows,
            out_rows,
            out_mem_rows,
            out_mem_rows,
            pl.BlockSpec((3 * width, 128), lambda p, *_: (0, first + p)),
            pl.BlockSpec((1, 8, basis), lambda p, *_: (first + p, 0, 0)),
            pl.BlockSpec((1, 16, 128), lambda p, *_: (first + p, 0, 0)),
        ],
        [shape_of((length, half), BF16)] * 3
        + [shape_of((basis, half), BF16)] * 2
        + [
            shape_of((3 * width, half), BF16),
            shape_of((side_pairs, 8, basis), F32),
            shape_of((side_pairs, 16, 128), F32),
        ],
        pairs * (28 * length * length * 128 + 6 * length * width * 128),
        "attend_back",
        operands + earlier,
        scalars=(scalars, flags),
        aliases={2 + len(operands) + index: index for index in range(len(earlier))},
    )


def feed_step(normed, normed_t, out_grad, up, up_bias, down, d_up, d_up_bias, d_down):
    weight_up = up[...]
    weight_down = down[...]
    before = dot_nn(normed[...], weight_up) + up_bias[...]
    out_rows = out_grad[...]
    hidden_grad = dot_nt(out_rows, weight_down)
    root = math.sqrt(2.0 / math.pi)
    square = before * before
    angle = jnp.tanh(before * (root + (root * 0.044715) * square))
    half_sum = 0.5 + 0.5 * angle
    activated = (before * half_sum).astype(BF16)
    slope = half_sum + before * (0.5 - 0.5 * angle * angle) * (
        root + (3.0 * 0.044715 * root) * square
    )
    before_grad = (hidden_grad * slope).astype(BF16)
    d_down[...] = dot_tn(activated, out_rows).astype(BF16)
    d_up[...] = dot_nn(normed_t[...], before_grad).astype(BF16)
    d_up_bias[...] = dot_nn(jnp.ones((8, before.shape[0]), BF16), before_grad)
    return dot_nn(activated, weight_down), dot_nt(before_grad, weight_up)


def residual_step(rows, mix, hid, wo, vectors, middle, normed, normed_t):
    branch = dot_nn(mix[rows, :], wo)
    values = hid[rows, :].astype(F32) + (branch + vectors[2:3])
    middle[rows, :] = values
    scaled, _ = scaled_rows(values)
    result = (scaled * vectors[3:4] + vectors[4:5]).astype(BF16)
    normed[rows, :] = result
    normed_t[:, rows] = result.T


def branch_step(rows, grad_sum, out_grad, middle, mix_t, wo, vectors, mid_grad, mix_grad):
    scaled, inverse = scaled_rows(middle[rows, :])
    grad_rows = grad_sum[rows, :]
    out_rows = out_grad[rows, :].astype(F32)
    result = out_rows + norm_back(grad_rows, scaled, inverse, vectors[3:4])
    mid_grad[rows, :] = result
    branch = result.astype(BF16)
    mix_grad[rows, :] = dot_nt(branch, wo).astype(BF16)
    sums = jnp.concatenate(
        [
            jnp.sum(branch.astype(F32), axis=0, keepdims=True),
            jnp.sum(grad_rows * scaled, axis=0, keepdims=True),
            jnp.sum(grad_rows, axis=0, keepdims=True),
            jnp.sum(out_rows, axis=0, keepdims=True),
            jnp.zeros((4, grad_rows.shape[1]), F32),
        ],
        axis=0,
    )
    return dot_nn(mix_t[:, rows], branch), sums


def feed_kernel(
    steps, scalars, mix, hid, mix_t, w_own, w_far, out_mine, out_theirs, vectors, up_far, up_own, ub_far,
    ub_own, down_far, down_own, du_far, du_own, dub_far, dub_own, dd_far, dd_own, mine, theirs, mid_grad,
    mix_grad, dw_own, dw_far, sums, middle, normed, normed_t, out_grad, out_sum, grad_sum, up, ub, down,
    du, dub, dd,
):
    index = pl.program_id(0)
    step = index - 1
    me = scalars[0]
    length = mix.shape[0]
    tokens = theirs.shape[0]
    spans = [slice(start, start + tokens) for start in range(0, length, tokens)]

    def half_at(half):
        return pl.ds(pl.multiple_of(half * tokens, tokens), tokens)

    @pl.when(index == 0)
    def _():
        out_sum[...] = jnp.zeros_like(out_sum)
        grad_sum[...] = jnp.zeros_like(grad_sum)
        out_grad[half_at(me), :] = out_mine[0]
        out_grad[half_at(1 - me), :] = out_theirs[...]
        wo = jnp.concatenate([w_own[...], w_far[...]], axis=0)
        for rows in spans:
            residual_step(rows, mix, hid, wo, vectors, middle, normed, normed_t)

    @pl.when((step >= 0) & (step < 2 * steps))
    def _():
        for side, weights in ((0, (up_far, ub_far, down_far)), (1, (up_own, ub_own, down_own))):

            @pl.when((step >= steps) == (side == 1))
            def _():
                for held, source in zip((up, ub, down), weights):
                    held[...] = source[...]

        forward, backward = feed_step(normed, normed_t, out_grad, up, ub, down, du, dub, dd)
        out_sum[...] += forward
        grad_sum[...] += backward
        for side, grads in ((0, (du_far, dub_far, dd_far)), (1, (du_own, dub_own, dd_own))):

            @pl.when((step >= steps) == (side == 1))
            def _():
                for target, held in zip(grads, (du, dub, dd)):
                    target[...] = held[...]

    @pl.when(step == 2 * steps)
    def _():
        for target, half in ((mine.at[0], me), (theirs, 1 - me)):
            at = half_at(half)
            target[...] = (middle[at, :] + out_sum[at, :] + vectors[5:6]).astype(BF16)
        wo = jnp.concatenate([w_own[...], w_far[...]], axis=0)
        total = None
        for rows in spans:
            fresh, added_sums = branch_step(
                rows, grad_sum, out_grad, middle, mix_t, wo, vectors, mid_grad, mix_grad
            )
            total = fresh if total is None else total + fresh
            sums[...] = added_sums if rows.start == 0 else sums[...] + added_sums
        half = w_own.shape[0]
        for side, out in enumerate((dw_own, dw_far)):
            rows = slice(side * half, (side + 1) * half)
            out[:half] = total[rows, :half].astype(BF16)
            out[half:] = total[rows, half:].astype(BF16)


def feed(order, scalars, mix, hid, mix_t, w_own, w_far, out_grad, out_grad_come, vectors, up_far, up_own, ub_far, ub_own, down_far, down_own):
    length, width = hid.shape
    tokens = length // 2
    hidden = up_own.shape[1]
    steps = hidden // FEED_BLOCK

    def far_block(i):
        return jnp.clip(i - 1, 0, steps - 1)

    def own_block(i):
        return jnp.clip(i - 1 - steps, 0, steps - 1)

    def up_spec(block):
        return pl.BlockSpec((width, FEED_BLOCK), lambda i, s: (0, block(i)))

    def bias_spec(block, rows):
        return pl.BlockSpec((rows, FEED_BLOCK), lambda i, s: (0, block(i)))

    def down_spec(block):
        return pl.BlockSpec((FEED_BLOCK, width), lambda i, s: (block(i), 0))

    def once(shape, place=None):
        zeros = (0,) * len(shape)
        return pl.BlockSpec(
            shape, place or (lambda i, s: zeros), pipeline_mode=pl.Buffered(1)
        )

    def mine_at(i, s):
        return (s[0], 0, 0)

    return order.call(
        functools.partial(feed_kernel, steps),
        (2 * steps + 2,),
        [
            once((length, width)),
            once((length, width)),
            once((width, length)),
            once(w_own.shape),
            once(w_far.shape),
            once((1, tokens, width), mine_at),
            once((tokens, width)),
            once(vectors.shape),
            up_spec(far_block),
            up_spec(own_block),
            bias_spec(far_block, 1),
            bias_spec(own_block, 1),
            down_spec(far_block),
            down_spec(own_block),
        ],
        [
            up_spec(far_block),
            up_spec(own_block),
            bias_spec(far_block, 8),
            bias_spec(own_block, 8),
            down_spec(far_block),
            down_spec(own_block),
            pl.BlockSpec((1, tokens, width), mine_at),
            whole((tokens, width)),
            whole((length, width)),
            whole((length, width)),
            whole((width, width // 2)),
            whole((width, width // 2)),
            whole((8, width)),
        ],
        [
            shape_of((width, hidden), BF16),
            shape_of((width, hidden), BF16),
            shape_of((8, hidden), F32),
            shape_of((8, hidden), F32),
            shape_of((hidden, width), BF16),
            shape_of((hidden, width), BF16),
            shape_of((2, tokens, width), BF16),
            shape_of((tokens, width), BF16),
            shape_of((length, width), F32),
            shape_of((length, width), BF16),
            shape_of((width, width // 2), BF16),
            shape_of((width, width // 2), BF16),
            shape_of((8, width), F32),
        ],
        24 * length * width * hidden,
        "feed",
        (mix, hid, mix_t, w_own, w_far, out_grad, out_grad_come, vectors)
        + (up_far, up_own, ub_far, ub_own, down_far, down_own),
        scratch=[
            pltpu.VMEM((length, width), F32),
            pltpu.VMEM((length, width), BF16),
            pltpu.VMEM((width, length), BF16),
            pltpu.VMEM((length, width), BF16),
            pltpu.VMEM((length, width), F32),
            pltpu.VMEM((length, width), F32),
            pltpu.VMEM((width, FEED_BLOCK), BF16),
            pltpu.VMEM((1, FEED_BLOCK), F32),
            pltpu.VMEM((FEED_BLOCK, width), BF16),
            pltpu.VMEM((width, FEED_BLOCK), BF16),
            pltpu.VMEM((8, FEED_BLOCK), F32),
            pltpu.VMEM((FEED_BLOCK, width), BF16),
        ],
        scalars=(scalars,),
    )


def input_back_kernel(
    scalars, hid, mid_grad, vectors, w_own, w_far, dq_own, dk_own, dv_own, dq_far, dk_far, dv_far,
    dmk_own, dmv_own, dmk_far, dmv_far, mine, theirs, coeff_mine, coeff_theirs, sums, total,
):
    me = scalars[0]
    index = pl.program_id(0)

    def back(own, far, part):
        return dot_nt(
            jnp.concatenate([own[...], far[...]], axis=1),
            jnp.concatenate([w_own[part], w_far[part]], axis=1),
        )

    grad_rows = back(dq_own, dq_far, 0) + back(dk_own, dk_far, 1) + back(dv_own, dv_far, 2)
    scaled, inverse = scaled_rows(hid[...].astype(F32))
    result = mid_grad[...] + norm_back(grad_rows, scaled, inverse, vectors[0:1])

    @pl.when(index == me)
    def _():
        mine[0] = result

    @pl.when(index != me)
    def _():
        theirs[...] = result.astype(BF16)

    fresh = jnp.concatenate(
        [
            jnp.sum(grad_rows * scaled, axis=0, keepdims=True),
            jnp.sum(grad_rows, axis=0, keepdims=True),
            jnp.zeros((6, grad_rows.shape[1]), F32),
        ],
        axis=0,
    )

    @pl.when(index == 0)
    def _():
        sums[...] = fresh
        total[...] = back(dmk_own, dmk_far, 1) + back(dmv_own, dmv_far, 2)
        part = coeff_theirs.shape[0]
        coeff_mine[0] = total[pl.ds(pl.multiple_of(me * part, part), part), :]
        coeff_theirs[...] = total[
            pl.ds(pl.multiple_of((1 - me) * part, part), part), :
        ].astype(BF16)

    @pl.when(index > 0)
    def _():
        sums[...] += fresh


def input_back(order, scalars, hid, mid_grad, vectors, w_own, w_far, own, far):
    length, width = hid.shape
    tokens = length // 2
    basis, half = own[3].shape
    rows = pl.BlockSpec((tokens, width), lambda i, s: (i, 0))
    half_rows = pl.BlockSpec((tokens, half), lambda i, s: (i, 0))
    return order.call(
        input_back_kernel,
        (2,),
        [rows, rows, whole(vectors.shape), whole(w_own.shape), whole(w_far.shape)]
        + [half_rows] * 6
        + [whole((basis, half))] * 4,
        [
            pl.BlockSpec((1, tokens, width), lambda i, s: (s[0], 0, 0)),
            whole((tokens, width)),
            pl.BlockSpec((1, basis // 2, width), lambda i, s: (s[0], 0, 0)),
            whole((basis // 2, width)),
            whole((8, width)),
        ],
        [
            shape_of((2, tokens, width), F32),
            shape_of((tokens, width), BF16),
            shape_of((2, basis // 2, width), F32),
            shape_of((basis // 2, width), BF16),
            shape_of((8, width), F32),
        ],
        6 * length * width * width,
        "input_back",
        (hid, mid_grad, vectors, w_own, w_far, *own[:3], *far[:3], *own[3:5], *far[3:5]),
        scratch=[pltpu.VMEM((basis, width), F32)],
        scalars=(scalars,),
    )


def tokens_place_kernel(scalars, *refs):
    for come, out in zip(refs[:3], refs[6:]):
        out[0] = come[...].astype(out.dtype)


def tokens_place(order, scalars, filled, come):
    return order.call(
        tokens_place_kernel,
        (1,),
        [whole(c.shape) for c in come] + [pl.BlockSpec(memory_space=pl.ANY)] * 3,
        [pl.BlockSpec((1,) + f.shape[1:], lambda i, s: (1 - s[0], 0, 0)) for f in filled],
        [shape_of(f.shape, f.dtype) for f in filled],
        0,
        "tokens_place",
        tuple(come) + tuple(filled),
        scalars=(scalars,),
        aliases={4 + index: index for index in range(3)},
    )


def pack_kernel(own_maps, own_sums, own_bias, far_maps, far_sums, far_bias, mid_sums, first_sums, own, far):
    for maps, sums, bias, out in (
        (own_maps, own_sums, own_bias, own),
        (far_maps, far_sums, far_bias, far),
    ):
        row = 0

        def put(values):
            nonlocal row
            for start in range(0, values.shape[1], 128):
                out[row : row + 1] = values[:, start : start + 128]
                row += 1

        for pair in range(maps.shape[0]):
            for index in range(4):
                put(maps[pair, index : index + 1])
        for index in (8, 9):
            for pair in range(maps.shape[0]):
                put(sums[pair, index : index + 1])
        put(bias[0:1])
        for index in range(4):
            put(mid_sums[index : index + 1])
        for index in range(2):
            put(first_sums[index : index + 1])
        for pair in range(maps.shape[0]):
            for index in range(4):
                put(sums[pair, index : index + 1])
        out[row:] = jnp.zeros((out.shape[0] - row, 128), F32)


def pack(order, own, own_bias, far, far_bias, mid_sums, first_sums):
    operands = (own[6], own[7], own_bias, far[6], far[7], far_bias, mid_sums, first_sums)
    pairs, _, basis = own[6].shape
    width = mid_sums.shape[1]
    count = pairs * 4 * (basis // 128) + 6 * pairs + own_bias.shape[1] // 128 + 6 * width // 128
    count += -count % 8
    return order.call(
        pack_kernel,
        (1,),
        [whole(o.shape) for o in operands],
        [whole((count, 128))] * 2,
        [shape_of((count, 128), F32)] * 2,
        0,
        "pack",
        operands,
    )


def to_peer(values):
    return jax.tree.map(lambda v: lax.ppermute(v, "mp", [(0, 1), (1, 0)]), values)


def across(values, offset, count):
    return lax.ppermute(values, "batch", [(i, i ^ offset) for i in range(count)])


def added(left, right):
    return left + right


def halve_kernel(flip, scalars, *refs):
    for chunk in range(2):
        low, high, low_more, high_more = refs[4 * chunk : 4 * chunk + 4]
        keep, send = refs[8 + 2 * chunk : 10 + 2 * chunk]
        bit = scalars[1 + (chunk ^ flip)]

        @pl.when(bit == 0)
        def _():
            keep[...] = added(low[...], low_more[...])
            send[...] = added(high[...], high_more[...])

        @pl.when(bit != 0)
        def _():
            keep[...] = added(high[...], high_more[...])
            send[...] = added(low[...], low_more[...])


def share_kernel(group, scalars, keep_a, more_a, keep_b, more_b, *outs):
    rows_a = keep_a.shape[0] // group
    rows_b = keep_b.shape[0] // group
    width = keep_b.shape[1]
    for offset in range(group):
        place = scalars[3 + offset]
        at = pl.ds(pl.multiple_of(place * rows_a, rows_a), rows_a)
        share = added(keep_a[at, :], more_a[at, :])
        for part in range(keep_a.shape[1] // width):
            outs[offset][part * rows_a : (part + 1) * rows_a] = share[
                :, part * width : (part + 1) * width
            ]
        at = pl.ds(pl.multiple_of(place * rows_b, rows_b), rows_b)
        outs[offset][outs[offset].shape[0] - rows_b :] = added(keep_b[at, :], more_b[at, :])


def total_kernel(*refs):
    total = refs[0][...].astype(F32)
    for ref in refs[1:-1]:
        total += ref[...].astype(F32)
    refs[-1][...] = total.astype(BF16)


def spread_kernel(group, scalars, *refs):
    out = refs[group]
    rows = out.shape[0] // group
    for offset in range(group):
        at = pl.ds(pl.multiple_of(scalars[3 + offset] * rows, rows), rows)
        out[at, :] = refs[offset][...]


def small_kernel(left, right, out):
    out[...] = left[...] + right[...]


def small_add(order, left, right):
    return order.call(
        small_kernel,
        (1,),
        [whole(left.shape)] * 2,
        [whole(left.shape)],
        [shape_of(left.shape, F32)],
        0,
        "small_add",
        (left, right),
    )[0]


class BatchSum:
    def __init__(self, order, scalars, count):
        self.order = order
        self.scalars = scalars
        self.count = count
        self.group = min(4, count // 4)

    def halve(self, flip, quads):
        specs = []
        operands = []
        out_specs = []
        shapes = []
        for shape, quad in quads:
            cuts = self.cuts(shape[0])
            piece = (shape[0] // cuts, shape[1])
            for values, block in quad:
                specs.append(
                    pl.BlockSpec(
                        piece, lambda i, s, block=block, cuts=cuts: (block[0] * cuts + i, block[1])
                    )
                )
                operands.append(values)
            out_specs += [pl.BlockSpec(piece, lambda i, s: (i, 0))] * 2
            shapes += [shape, shape]
        keep_a, send_a, keep_b, send_b = self.order.call(
            functools.partial(halve_kernel, flip),
            (cuts,),
            specs,
            out_specs,
            [shape_of(s, BF16) for s in shapes],
            0,
            "halve",
            operands,
            scalars=(self.scalars,),
        )
        self.kept = (keep_a, keep_b)
        self.come = (
            across(send_a, 1 << flip, self.count),
            across(send_b, 2 >> flip, self.count),
        )

    def cuts(self, rows):
        return 4 if rows % 64 == 0 else 1

    def first(self, quads):
        self.halve(0, quads)

    def second(self):
        quads = []
        for kept, come in zip(self.kept, self.come):
            shape = (kept.shape[0] // 2, kept.shape[1])
            quads.append((shape, ((kept, (0, 0)), (kept, (1, 0)), (come, (0, 0)), (come, (1, 0)))))
        self.halve(1, quads)

    def around(self, own):
        return [own[0]] + [
            across(own[offset], offset << 2, self.count) for offset in range(1, self.group)
        ]

    def share(self):
        operands = (self.kept[0], self.come[0], self.kept[1], self.come[1])
        width = operands[2].shape[1]
        shape = ((operands[0].size + operands[2].size) // (width * self.group), width)
        self.shares = self.around(
            self.order.call(
                functools.partial(share_kernel, self.group),
                (1,),
                [whole(o.shape) for o in operands],
                [whole(shape)] * self.group,
                [shape_of(shape, BF16)] * self.group,
                0,
                "share",
                operands,
                scalars=(self.scalars,),
            )
        )

    def total(self):
        shape = self.shares[0].shape
        (self.mine,) = self.order.call(
            total_kernel,
            (1,),
            [whole(shape)] * self.group,
            [whole(shape)],
            [shape_of(shape, BF16)],
            0,
            "total",
            self.shares,
        )
        offset = 4 * self.group
        while offset < self.count:
            self.mine = added(self.mine, across(self.mine, offset, self.count))
            offset *= 2

    def around_rest(self):
        self.pieces = self.around([self.mine] * self.group)

    def spread(self):
        rows, width = self.mine.shape
        shape = (self.group * rows, width)
        (quarter,) = self.order.call(
            functools.partial(spread_kernel, self.group),
            (1,),
            [whole(p.shape) for p in self.pieces],
            [whole(shape)],
            [shape_of(shape, BF16)],
            0,
            "spread",
            self.pieces,
            scalars=(self.scalars,),
        )
        self.quarters = [quarter] + [
            across(quarter, offset, self.count) for offset in (1, 2, 3)
        ]


def peers_added_kernel(*refs):
    for index in range(2):
        refs[4 + index][...] = added(refs[2 * index][...], refs[2 * index + 1][...])
    refs[6][...] = jnp.zeros_like(refs[6])


def peers_added(order, up_pair, down_pair):
    cuts = 4
    width = down_pair[0].shape[1]
    up_spec = pl.BlockSpec((up_pair[0].shape[0] // cuts, width), lambda i: (i, 1))
    up_out = pl.BlockSpec((up_pair[0].shape[0] // cuts, width), lambda i: (i, 0))
    down_spec = pl.BlockSpec((down_pair[0].shape[0] // cuts, width), lambda i: (i, 0))
    return order.call(
        peers_added_kernel,
        (cuts,),
        [up_spec, up_spec, down_spec, down_spec],
        [up_out, down_spec, whole((8, 128))],
        [
            shape_of((up_pair[0].shape[0], width), BF16),
            shape_of(down_pair[0].shape, BF16),
            shape_of((8, 128), F32),
        ],
        0,
        "peers_added",
        tuple(up_pair) + tuple(down_pair),
    )[:2]


def feed_place_kernel(up_sum, down_sum, _, up_out, down_out):
    up_out[...] = up_sum[...].astype(F32)
    down_out[...] = down_sum[...].astype(F32)


def feed_place(order, up_sum, down_sum, up_grad):
    cuts = 4
    width = down_sum.shape[1]
    up_rows = up_sum.shape[0] // cuts
    down_rows = down_sum.shape[0] // cuts
    return order.call(
        feed_place_kernel,
        (cuts,),
        [
            pl.BlockSpec((up_rows, width), lambda i: (i, 0)),
            pl.BlockSpec((down_rows, width), lambda i: (i, 0)),
            pl.BlockSpec(memory_space=pl.ANY),
        ],
        [
            pl.BlockSpec((up_rows, width), lambda i: (i, 1)),
            pl.BlockSpec((down_rows, width), lambda i: (i, 0)),
        ],
        [shape_of(up_grad.shape, F32), shape_of(down_sum.shape, F32)],
        0,
        "feed_place",
        (up_sum, down_sum, up_grad),
        aliases={2: 0},
    )


def mixed_halve_kernel(scalars, *refs):
    for chunk in range(2):
        keep, send = refs[16 + 2 * chunk : 18 + 2 * chunk]
        bit = scalars[1 + chunk]

        def fill(target, half):
            own, own_more, peer, peer_more = refs[8 * chunk + 4 * half : 8 * chunk + 4 * half + 4]
            rows = own.shape[0]
            target[:rows] = added(own[...], peer[...])
            target[rows:] = added(own_more[...], peer_more[...])

        @pl.when(bit == 0)
        def _():
            fill(keep, 0)
            fill(send, 1)

        @pl.when(bit != 0)
        def _():
            fill(keep, 1)
            fill(send, 0)


class MixedSum(BatchSum):
    def first(self, dqkv, dwo, du):
        width, cols = dwo[0].shape
        part = width // 2
        steps = cols // 128
        specs = []
        operands = []
        for chunk in range(2):
            for half in range(2):
                main = dwo if (chunk, half) == (1, 1) else dqkv
                block = 0 if main is dwo else 2 * chunk + half
                for side in range(2):
                    specs.append(pl.BlockSpec((width, 128), lambda i, s, b=block: (b, i)))
                    specs.append(
                        pl.BlockSpec((part, 128), lambda i, s, h=half, c=chunk: (h, steps * c + i))
                    )
                    operands += [main[side], du[side]]
        shape = (width + part, cols)
        keep_a, send_a, keep_b, send_b = self.order.call(
            mixed_halve_kernel,
            (steps,),
            specs,
            [pl.BlockSpec((width + part, 128), lambda i, s: (0, i))] * 4,
            [shape_of(shape, BF16)] * 4,
            0,
            "mixed_halve",
            operands,
            scalars=(self.scalars,),
        )
        self.kept = (keep_a, keep_b)
        self.come = (across(send_a, 1, self.count), across(send_b, 2, self.count))


def mixed_place_kernel(group, scalars, *refs):
    qkv_out, up_out, wo_out = refs[-3:]
    cols = refs[0].shape[1]
    width = wo_out.shape[1]
    part = width // 2
    rows = refs[0].shape[0] // (2 * group)

    def segments(quarter, place):
        start = (quarter * group + place) * rows
        marks = [start] + [m for m in (part, width) if start < m < start + rows] + [start + rows]
        return [(a, a - start, b - a) for a, b in zip(marks, marks[1:])]

    for index in range(4):
        column = scalars[1] ^ (index % 2)
        row = scalars[2] ^ (index // 2)
        values = refs[index]
        for quarter in range(2):

            @pl.when(row == quarter)
            def _():
                for place in range(group):
                    for at, inner, size in segments(quarter, place):
                        start = 2 * place * rows + inner
                        piece = values[start : start + size].astype(F32)
                        if at < width:
                            to = pl.multiple_of(column * width + at, 16)
                            qkv_out[pl.ds(to, size), :] = piece
                        else:
                            to = pl.multiple_of(column * part + at - width, 16)
                            up_out[pl.ds(to, size), :cols] = piece

            for half in range(2):

                @pl.when((column == quarter) & (row == half))
                def _():
                    for place in range(group):
                        for at, inner, size in segments(quarter, place):
                            start = (2 * place + 1) * rows + inner
                            piece = values[start : start + size].astype(F32)
                            if at >= width:
                                to = half * part + at - width
                                up_out[to : to + size, cols:] = piece
                            elif half == 0:
                                qkv_out[2 * width + at : 2 * width + at + size] = piece
                            elif at < part:
                                wo_out[at : at + size, :cols] = piece
                            else:
                                wo_out[at - part : at - part + size, cols:] = piece


def mixed_place(order, scalars, summed, width, hidden):
    half = width // 2
    return order.call(
        functools.partial(mixed_place_kernel, summed.group),
        (1,),
        [whole(o.shape) for o in summed.quarters],
        [
            whole((3 * width, half)),
            pl.BlockSpec((width, width), lambda i, s: (0, 0)),
            whole((half, width)),
        ],
        [
            shape_of((3 * width, half), F32),
            shape_of((width, hidden), F32),
            shape_of((half, width), F32),
        ],
        0,
        "mixed_place",
        summed.quarters,
        scalars=(scalars,),
    )


def per_device(
    count,
    hidden_in,
    memory_flags,
    memory_coeffs,
    first_gain,
    first_bias,
    query_key_value_matrix,
    qv_bias,
    memory_weight,
    memory_bias,
    output_matrix,
    out_bias,
    second_gain,
    second_bias,
    up_matrix,
    up_bias_vector,
    down_matrix,
    down_bias,
    out_grad,
):
    me = lax.axis_index("mp")
    position = lax.axis_index("batch")
    width = hidden_in.shape[2]
    half = width // 2
    group = min(4, count // 4)
    place = (position >> 2) % group
    scalars = jnp.stack(
        [me, position & 1, (position >> 1) & 1] + [place ^ offset for offset in range(group)]
    ).astype(jnp.int32)

    def from_peer(values):
        return to_peer(lax.dynamic_index_in_dim(values, 1 - me, 0, keepdims=False))

    hidden_come = from_peer(hidden_in)
    w_own = jnp.transpose(query_key_value_matrix, (1, 0, 2))
    w_far = to_peer(w_own)
    coeffs_come = from_peer(memory_coeffs)
    qv_far, mw_far, mb_far, ub_far = to_peer(
        (qv_bias, memory_weight, memory_bias, up_bias_vector)
    )

    query_bias = jnp.concatenate([qv_bias, qv_far], axis=1).astype(F32)
    mem_maps = jnp.concatenate([memory_weight, mw_far], axis=1).astype(F32)
    mem_maps = jnp.transpose(mem_maps, (1, 0, 2))
    mem_biases = jnp.concatenate([memory_bias, mb_far], axis=1).astype(F32)
    vectors = jnp.stack(
        [first_gain, first_bias, out_bias, second_gain, second_bias, down_bias] + [down_bias] * 2
    )
    order = Order()
    hid, norm_t, q, k, v, mem_k, mem_v, coeffs_t = project(
        order, scalars, hidden_in, hidden_come, vectors, w_own, w_far, query_bias, memory_coeffs, coeffs_come
    )
    later, _ = lax.optimization_barrier(
        ((output_matrix, out_grad, up_matrix, down_matrix), (coeffs_t, mw_far, mb_far, ub_far))
    )
    wo_far = to_peer(later[0])
    out_grad_come = from_peer(later[1])
    up_far = to_peer(later[2])
    down_far = to_peer(later[3])
    att_t, mix_t, mix, stat = attend(
        order, scalars, memory_flags, q, k, v, mem_k, mem_v, mem_maps, mem_biases
    )
    (
        du_far,
        du_own,
        dub_far,
        dub_own,
        dd_far,
        dd_own,
        block_mine,
        block_theirs,
        mid_grad,
        mix_grad,
        dwo_own,
        dwo_far,
        mid_sums,
    ) = feed(
        order,
        scalars,
        mix,
        hid,
        mix_t,
        output_matrix,
        wo_far,
        out_grad,
        out_grad_come,
        vectors,
        up_far,
        up_matrix,
        ub_far.astype(F32)[None],
        up_bias_vector.astype(F32)[None],
        down_far,
        down_matrix,
    )
    du_peer, dd_peer = to_peer((du_far, dd_far))
    dwo_peer = to_peer(dwo_far)
    back_args = (
        scalars, memory_flags, q, k, v, mem_k, mem_v, mem_maps, mix_grad, att_t, stat, norm_t, coeffs_t
    )
    pairs = width // 256
    far = attend_back(order, 1, 0, pairs, None, *back_args)
    up_sum, down_sum = peers_added(order, (du_own, du_peer), (dd_own, dd_peer))
    dqkv_peer = to_peer(far[5])
    up_sum, down_sum = lax.psum((up_sum, down_sum), "batch")
    block_come = to_peer(block_theirs)
    own = attend_back(order, 0, 0, pairs, None, *back_args)
    dqkv_own = own[5]
    last = MixedSum(order, scalars, count)
    last.first((dqkv_own, dqkv_peer), (dwo_own, dwo_peer), (du_own, du_peer))
    in_mine, in_theirs, coeff_mine, coeff_theirs, first_sums = input_back(
        order, scalars, hid, mid_grad, vectors, w_own, w_far, own, far
    )
    small, far_flat = pack(order, own, dub_own, far, dub_far, mid_sums, first_sums)
    last.second()
    come, in_come, coeff_come = to_peer(
        lax.optimization_barrier((far_flat, in_theirs, coeff_theirs, last.kept[0]))[:3]
    )
    block_out, input_grad, coeff_grad = tokens_place(
        order, scalars, (block_mine, in_mine, coeff_mine), (block_come, in_come, coeff_come)
    )
    last.share()
    small = small_add(order, small, come)
    small = small_add(order, small, across(small, 1, count))
    last.total()
    last.around_rest()
    small = small_add(order, small, across(small, 2, count))
    last.spread()
    offset = 4
    while offset < count:
        small = small_add(order, small, across(small, offset, count))
        offset *= 2
    query_key_value_grad, up_weight_grad, output_matrix_grad = mixed_place(
        order, scalars, last, width, up_matrix.shape[1]
    )
    query_key_value_grad = jnp.transpose(
        query_key_value_grad.reshape(3, width, half), (1, 0, 2)
    )
    up_weight_grad, down_weight_grad = feed_place(order, up_sum, down_sum, up_weight_grad)

    heads, basis = memory_weight.shape[1:]
    rows = 0

    def take(size):
        nonlocal rows
        piece = small[rows : rows + size // 128]
        rows += size // 128
        return piece

    memory_weight_grad = jnp.transpose(take(2 * heads * basis).reshape(heads, 2, basis), (1, 0, 2))
    qv_bias_grad = take(2 * half).reshape(2, half)
    up_bias_grad = take(up_bias_vector.shape[0]).reshape(-1)
    vector_grads = [take(width).reshape(-1) for _ in range(6)]
    memory_bias_grad = jnp.transpose(take(2 * heads * 128)[:, 0].reshape(heads, 2), (1, 0))
    return (
        block_out,
        input_grad,
        coeff_grad,
        vector_grads[4],
        vector_grads[5],
        query_key_value_grad,
        qv_bias_grad,
        memory_weight_grad,
        memory_bias_grad,
        output_matrix_grad,
        vector_grads[0],
        vector_grads[1],
        vector_grads[2],
        up_weight_grad,
        up_bias_grad,
        down_weight_grad,
        vector_grads[3],
    )


def solution(mesh):
    tokens = P("batch", "mp", None)
    return jax.shard_map(
        functools.partial(per_device, mesh.shape["batch"]),
        mesh=mesh,
        in_specs=(
            tokens,
            P("batch"),
            tokens,
            P(),
            P(),
            P(None, None, "mp"),
            P(None, "mp"),
            P(None, "mp", None),
            P(None, "mp"),
            P("mp", None),
            P(),
            P(),
            P(),
            P(None, "mp"),
            P("mp"),
            P("mp", None),
            P(),
            tokens,
        ),
        out_specs=(
            tokens,
            tokens,
            tokens,
            P(),
            P(),
            P(None, None, "mp"),
            P(None, "mp"),
            P(None, "mp", None),
            P(None, "mp"),
            P("mp", None),
            P(),
            P(),
            P(),
            P(None, "mp"),
            P("mp"),
            P("mp", None),
            P(),
        ),
        check_vma=False,
    )
```

profile of v0, /device:TPU:0, one launch (start us, length us, event | category | flops | bytes accessed | tf_op | source)
XLA Modules:
  0.0 360.7 jit_solution(9155450972707857479)
XLA Ops:
  7.9 1.2 dynamic-slice_bitcast_fusion.1
  9.2 0.9 dynamic-slice_bitcast_fusion.2
  13.8 1.2 copy-done.4
  15.0 11.5 %project.1 = (bf16[1024,768]{1,0:T(8,128)(2,1)}, bf16[768,1024]{1,0:T(8,128)(2,1)}, bf16[1024,768]{1,0:T(8,128)(2,1)}, bf16[1024,768]{1,0:T(8,128)(2,1)}, bf16[1...) custom-call(s32[7]{0:T(128)} %stack.54.refs_0_, ...), custom_call_target="tpu_custom_call" | custom-call | flops 3623878656 | bytes 18087936 | tf_op jit(solution)/shard_map/project/pallas_call | solution.py:88
  30.3 18.7 %attend.1 = (f32[768,1024]{1,0:T(8,128)}, bf16[768,1024]{1,0:T(8,128)(2,1)}, bf16[1024,768]{1,0:T(8,128)(2,1)}, f32[48,1024]{1,0:T(8,128)}) custom-call(s32[7]{0:T(128)} %stack.54.refs_0_, s32[2]{0:T(128)} %refs_1_.7, bf16[1024,768]{1,0:T(8,128)(2,1)} %get-tuple-element.95.refs_2_, bf16[1024,768]{1,0:T(8,128)(2,1)} %get-tuple-element.96.refs_3_, ...), custom_call_target="tpu_custom_call" | custom-call | flops 9663676416 | bytes 12976128 | tf_op jit(solution)/shard_map/attend/pallas_call | solution.py:88
  49.0 0.8 copy-done.42
  49.9 0.8 copy-done.39
  50.6 65.5 %feed.1 = (bf16[768,1536]{1,0:T(8,128)(2,1)}, bf16[768,1536]{1,0:T(8,128)(2,1)}, f32[8,1536]{1,0:T(8,128)}, f32[8,1536]{1,0:T(8,128)}, bf16[1536,768]{1,0:T(8,12...) custom-call(s32[7]{0:T(128)} %stack.54.refs_0_, ...), custom_call_target="tpu_custom_call" | custom-call | flops 28991029248 | bytes 35635200 | tf_op jit(solution)/shard_map/feed/pallas_call | solution.py:88
  116.7 22.0 %attend_back.2 = (bf16[1024,384]{1,0:T(8,128)(2,1)}, bf16[1024,384]{1,0:T(8,128)(2,1)}, bf16[1024,384]{1,0:T(8,128)(2,1)}, bf16[256,384]{1,0:T(8,128)(2,1)}, bf1...) custom-call(s32[7]{0:T(128)} %stack.54.refs_0_, s32[2]{0:T(128)} %refs_1_.7, ...), custom_call_target="tpu_custom_call" | custom-call | flops 13086228480 | bytes 9142272 | tf_op jit(solution)/shard_map/attend_back/pallas_call | solution.py:88
  139.4 1.4 copy-done
  140.7 0.8 copy-done.3
  141.5 5.2 %peers_added.1 = (bf16[768,768]{1,0:T(8,128)(2,1)}, bf16[1536,768]{1,0:T(8,128)(2,1)}, f32[8,128]{1,0:T(8,128)}) custom-call(bf16[768,1536]{1,0:T(8,128)(2,1)} %get-tuple-element.113.refs_0_.refs_2_.refs_6_.refs_10_.refs_14_, bf16[768,1536]{1,0:T(8,128)(2,1)} %copy-done, bf16[1536,768]{1,0:T(8,128)(2,1)} %get-tuple-element.115.refs_2_, ...), custom_call_target="tpu_custom_call" | custom-call | bytes 7086080 | tf_op jit(solution)/shard_map/peers_added/pallas_call | solution.py:88
  146.7 21.8 %attend_back.3 = (bf16[1024,384]{1,0:T(8,128)(2,1)}, bf16[1024,384]{1,0:T(8,128)(2,1)}, bf16[1024,384]{1,0:T(8,128)(2,1)}, bf16[256,384]{1,0:T(8,128)(2,1)}, bf1...) custom-call(s32[7]{0:T(128)} %stack.54.refs_0_, s32[2]{0:T(128)} %refs_1_.7, ...), custom_call_target="tpu_custom_call" | custom-call | flops 13086228480 | bytes 9142272 | tf_op jit(solution)/shard_map/attend_back/pallas_call | solution.py:88
  168.6 0.8 copy-done.10
  169.4 6.9 %mixed_halve.1 = (bf16[1152,384]{1,0:T(8,128)(2,1)}, bf16[1152,384]{1,0:T(8,128)(2,1)}, bf16[1152,384]{1,0:T(8,128)(2,1)}, bf16[1152,384]{1,0:T(8,128)(2,1)}) custom-call(s32[7]{0:T(128)} %stack.54.refs_0_, bf16[2304,384]{1,0:T(8,128)(2,1)} %get-tuple-element.136.refs_1_.refs_5_.refs_9_, ...), custom_call_target="tpu_custom_call" | custom-call | bytes 7077888 | tf_op jit(solution)/shard_map/mixed_halve/pallas_call | solution.py:88
  176.2 2.8 collective-permute-start.16
  179.0 1.5 collective-permute-start.17
  180.6 13.3 %input_back.1 = (f32[2,512,768]{2,1,0:T(8,128)}, bf16[512,768]{1,0:T(8,128)(2,1)}, f32[2,128,768]{2,1,0:T(8,128)}, bf16[128,768]{1,0:T(8,128)(2,1)}, f32[8,768]{1,0:T(8,128)}) custom-call(s32[7]{0:T(128)} %stack.54.refs_0_, bf16[1024,768]{1,0:T(8,128)(2,1)} %get-tuple-element.102.refs_2_.refs_1_, f32[1024,768]{1,0:T(8,128)} %get-tuple-element.125.refs_2_, ...), custom_call_target="tpu_custom_call" | custom-call | flops 3623878656 | bytes 9879552 | tf_op jit(solution)/shard_map/input_back/pallas_call | solution.py:88
  193.9 1.6 pack.1
  195.5 8.5 %collective-permute-done.16.refs_3_.refs_4_ = bf16[1152,384]{1,0:T(8,128)(2,1)S(1)} collective-permute-done((bf16[1152,384]{1,0:T(8,128)(2,1)}, bf16[1152,384]{1,0:T(8,128)(2,1)S(1)}, u32[]{:S(2)}, u32[]{:S(2)}) %collective-permute-start.16) | collective-permute-done | bytes 884768 | tf_op jit(solution)/shard_map/ppermute | solution.py:870
  204.0 1.5 collective-permute-done.17.refs_7_.refs_8_
  205.5 0.9 copy-done.2
  206.4 5.1 %halve.1 = (bf16[576,384]{1,0:T(8,128)(2,1)}, bf16[576,384]{1,0:T(8,128)(2,1)}, bf16[576,384]{1,0:T(8,128)(2,1)}, bf16[576,384]{1,0:T(8,128)(2,1)}) custom-call(s32[7]{0:T(128)} %stack.54.refs_0_, bf16[1152,384]{1,0:T(8,128)(2,1)} %get-tuple-element.145.refs_1_.refs_2_, bf16[1152,384]{1,0:T(8,128)(2,1)} %get-tuple-element.145.refs_1_.refs_2_, ...), custom_call_target="tpu_custom_call" | custom-call | bytes 3538944 | tf_op jit(solution)/shard_map/halve/pallas_call | solution.py:88
  211.6 1.6 collective-permute-start.21
  213.8 1.4 collective-permute-done.19.refs_3_
  215.2 0.7 copy-done.21
  216.2 3.8 %tokens_place.1 = (bf16[2,512,768]{2,1,0:T(8,128)(2,1)}, f32[2,512,768]{2,1,0:T(8,128)}, f32[2,128,768]{2,1,0:T(8,128)}) custom-call(s32[7]{0:T(128)} %stack.54.refs_0_, bf16[512,768]{1,0:T(8,128)(2,1)} %copy-done.8, bf16[512,768]{1,0:T(8,128)(2,1)} %copy-done.9, ...), custom_call_target="tpu_custom_call", output_to_operand_aliasing={{0}: (4, {}), {1}: (5, {}), {2}: (6, {})} | custom-call | bytes 11010048 | tf_op jit(solution)/shard_map/tokens_place/pallas_call | solution.py:88
  220.0 6.9 %collective-permute-done.21.refs_2_ = bf16[576,384]{1,0:T(8,128)(2,1)S(1)} collective-permute-done((bf16[576,384]{1,0:T(8,128)(2,1)}, bf16[576,384]{1,0:T(8,128)(2,1)S(1)}, u32[]{:S(2)}, u32[]{:S(2)}) %collective-permute-start.21) | collective-permute-done | bytes 442400 | tf_op jit(solution)/shard_map/ppermute | solution.py:870
  226.9 0.8 copy-done.12
  227.8 3.1 share.1
  230.9 1.5 collective-permute-start.25
  232.4 2.6 collective-permute-start.26
  235.3 1.2 collective-permute-done.20.refs_1_
  237.1 1.4 small_add.5.refs_0_.refs_2_
  239.2 4.0 %collective-permute-done.23.refs_1_ = f32[96,128]{1,0:T(8,128)S(1)} collective-permute-done((f32[96,128]{1,0:T(8,128)}, f32[96,128]{1,0:T(8,128)S(1)}, u32[]{:S(2)}, u32[]{:S(2)}) %collective-permute-start.23) | collective-permute-done | bytes 49184 | tf_op jit(solution)/shard_map/ppermute | solution.py:870
  243.8 1.4 small_add.6.refs_4_.refs_0_
  245.3 8.4 %collective-permute-done.26.refs_2_ = bf16[288,384]{1,0:T(8,128)(2,1)S(1)} collective-permute-done((bf16[288,384]{1,0:T(8,128)(2,1)}, bf16[288,384]{1,0:T(8,128)(2,1)S(1)}, u32[]{:S(2)}, u32[]{:S(2)}) %collective-permute-start.26) | collective-permute-done | bytes 221216 | tf_op jit(solution)/shard_map/ppermute | solution.py:870
  253.7 0.7 copy-done.16
  254.5 2.1 total.1.refs_2_.refs_1_
  256.5 2.4 collective-permute-start.31
  258.9 6.5 %collective-permute-start.30 = (bf16[288,384]{1,0:T(8,128)(2,1)}, bf16[288,384]{1,0:T(8,128)(2,1)S(1)}, u32[]{:S(2)}, u32[]{:S(2)}) collective-permute-start(bf16[288,384]{1,0:T(8,128)(2,1)} %total.1.refs_2_.refs_1_), channel_id=1, source_target_pairs={{0,16},{2,18},{4,20},{6,22},{8,24},{10,26},{12,28},{14,30},{16,0},... | collective-permute-start | bytes 663560 | tf_op jit(solution)/shard_map/ppermute | solution.py:870
  265.4 1.3 collective-permute-start.24
  266.7 3.9 %collective-permute-done.24.refs_1_ = f32[96,128]{1,0:T(8,128)S(1)} collective-permute-done((f32[96,128]{1,0:T(8,128)}, f32[96,128]{1,0:T(8,128)S(1)}, u32[]{:S(2)}, u32[]{:S(2)}) %collective-permute-start.24) | collective-permute-done | bytes 49184 | tf_op jit(solution)/shard_map/ppermute | solution.py:870
  271.2 1.4 small_add.7.refs_5_.refs_0_
  272.6 13.3 %collective-permute-done.30.refs_3_ = bf16[288,384]{1,0:T(8,128)(2,1)S(1)} collective-permute-done((bf16[288,384]{1,0:T(8,128)(2,1)}, bf16[288,384]{1,0:T(8,128)(2,1)S(1)}, u32[]{:S(2)}, u32[]{:S(2)}) %collective-permute-start.30) | collective-permute-done | bytes 221216 | tf_op jit(solution)/shard_map/ppermute | solution.py:870
  285.9 0.7 copy-done.19
  286.6 0.7 copy-done.20
  287.3 3.0 spread.1.refs_2_.refs_1_
  290.2 1.4 collective-permute-start.35
  292.1 1.6 collective-permute-start.33
  293.7 7.5 %collective-permute-done.28.refs_1_ = f32[96,128]{1,0:T(8,128)S(1)} collective-permute-done((f32[96,128]{1,0:T(8,128)S(1)}, f32[96,128]{1,0:T(8,128)S(1)}, u32[]{:S(2)}, u32[]{:S(2)}) %collective-permute-start.28) | collective-permute-done | bytes 49184 | tf_op jit(solution)/shard_map/ppermute | solution.py:870
  301.9 1.4 small_add.8.refs_0_.refs_2_
  303.3 7.2 %collective-permute-done.32.refs_1_ = f32[96,128]{1,0:T(8,128)S(1)} collective-permute-done((f32[96,128]{1,0:T(8,128)}, f32[96,128]{1,0:T(8,128)S(1)}, u32[]{:S(2)}, u32[]{:S(2)}) %collective-permute-start.32) | collective-permute-done | bytes 49184 | tf_op jit(solution)/shard_map/ppermute | solution.py:870
  311.2 1.4 small_add.9.refs_5_
  312.6 0.7 slice.45
  313.3 0.8 slice_reduce_fusion
  315.5 1.4 slice_bitcast_fusion.1
  317.5 1.3 slice_bitcast_fusion
  318.8 3.7 %collective-permute-done.35.refs_4_ = bf16[1152,384]{1,0:T(8,128)(2,1)S(1)} collective-permute-done((bf16[1152,384]{1,0:T(8,128)(2,1)}, bf16[1152,384]{1,0:T(8,128)(2,1)S(1)}, u32[]{:S(2)}, u32[]{:S(2)}) %collective-permute-start.35) | collective-permute-done | bytes 884768 | tf_op jit(solution)/shard_map/ppermute | solution.py:870
  322.5 17.8 %collective-permute-done.34.refs_3_ = bf16[1152,384]{1,0:T(8,128)(2,1)S(1)} collective-permute-done((bf16[1152,384]{1,0:T(8,128)(2,1)}, bf16[1152,384]{1,0:T(8,128)(2,1)S(1)}, u32[]{:S(2)}, u32[]{:S(2)}) %collective-permute-start.34) | collective-permute-done | bytes 884768 | tf_op jit(solution)/shard_map/ppermute | solution.py:870
  340.3 0.9 copy-done.6
  341.2 0.9 copy-done.7
  342.2 6.2 %mixed_place.1 = (f32[2304,384]{1,0:T(8,128)}, f32[768,1536]{1,0:T(8,128)}, f32[384,768]{1,0:T(8,128)}) custom-call(s32[7]{0:T(128)} %stack.54.refs_0_, bf16[1152,384]{1,0:T(8,128)(2,1)} %spread.1.refs_2_.refs_1_, bf16[1152,384]{1,0:T(8,128)(2,1)} %copy-done.7, bf16[1152,384]{1,0:T(8,128)(2,1)} %copy-done.6, bf16[1152,384]{1,0:T(8,128)(2,1)} %copy-done.5, ...), custom_call_target="tpu_custom_call" | custom-call | bytes 18874368 | tf_op jit(solution)/shard_map/mixed_place/pallas_call | solution.py:88
  348.3 5.3 %feed_place.1 = (f32[768,1536]{1,0:T(8,128)}, f32[1536,768]{1,0:T(8,128)}) custom-call(bf16[768,768]{1,0:T(8,128)(2,1)} %get-tuple-element.207.refs_0_, bf16[1536,768]{1,0:T(8,128)(2,1)} %get-tuple-element.208.refs_1_, f32[768,1536]{1,0:T(8,128)} %get-tuple-element.170.refs_2_, f32[384,768]{1,0:T(8,128)} %get-tuple-element.199.refs_3_), custom_call_target="tpu_custom_call", output_to_operand_aliasing={{0}: (2, {})} | custom-call | bytes 18874368 | tf_op jit(solution)/shard_map/feed_place/pallas_call | solution.py:88
  (148 shorter events, 16.8 us)
Async XLA Ops:
  7.2 3.4 copy-start.37
  7.2 3.5 copy-start.36
  7.2 3.9 %copy-start.29 = (f32[768]{0:T(1024)S(1)}, f32[768]{0:T(1024)}, u32[]{:S(2)}) copy-start(f32[768]{0:T(1024)} %param.21) | copy-start | bytes 9220
  7.2 3.9 %copy-start.30 = (f32[768]{0:T(1024)S(1)}, f32[768]{0:T(1024)}, u32[]{:S(2)}) copy-start(f32[768]{0:T(1024)} %param.22) | copy-start | bytes 9220
  7.2 3.9 %copy-start.31 = (f32[768]{0:T(1024)S(1)}, f32[768]{0:T(1024)}, u32[]{:S(2)}) copy-start(f32[768]{0:T(1024)} %param.28) | copy-start | bytes 9220
  7.2 3.9 %copy-start.32 = (f32[768]{0:T(1024)S(1)}, f32[768]{0:T(1024)}, u32[]{:S(2)}) copy-start(f32[768]{0:T(1024)} %param.29) | copy-start | bytes 9220
  7.3 4.0 %copy-start.33 = (f32[768]{0:T(1024)S(1)}, f32[768]{0:T(1024)}, u32[]{:S(2)}) copy-start(f32[768]{0:T(1024)} %param.30) | copy-start | bytes 9220
  7.3 4.0 %copy-start.34 = (f32[768]{0:T(1024)S(1)}, f32[768]{0:T(1024)}, u32[]{:S(2)}) copy-start(f32[768]{0:T(1024)} %param.34) | copy-start | bytes 9220
  7.3 5.3 %copy-start.35 = (bf16[1536]{0:T(1024)(128)(2,1)S(1)}, bf16[1536]{0:T(1024)(128)(2,1)}, u32[]{:S(2)}) copy-start(bf16[1536]{0:T(1024)(128)(2,1)} %param.32) | copy-start | bytes 9220
  7.3 6.3 %copy-start.28 = (bf16[2,6,256]{2,0,1:T(2,128)(2,1)S(1)}, bf16[2,6,256]{2,0,1:T(2,128)(2,1)}, u32[]{:S(2)}) copy-start(bf16[2,6,256]{2,0,1:T(2,128)(2,1)} %param.25) | copy-start | bytes 18436
  7.3 341.0 %all-reduce.3.cloned.1.call-start = ((), (), s32[]{:S(2)}) async-start(), calls=%async_computation | async-start | bytes 7077888 | tf_op jit(solution)/shard_map/psum | solution.py:1348
  7.3 6.5 %collective-permute-start.1 = (bf16[3,768,384]{2,1,0:T(8,128)(2,1)}, bf16[3,768,384]{2,1,0:T(8,128)(2,1)S(1)}, u32[]{:S(2)}, u32[]{:S(2)}) collective-permute-start(bf16[3,768,384]{2,1,0:T(8,128)(2,1)} %bitcast.35), channel_id=1, source_target_pairs={{0,1},{1,0},{2,3},{3,2},{4,5},{5,4},{6,7},{7,6},{8,9},{9,8},{10,11... | collective-permute-start | bytes 5308424 | tf_op jit(solution)/shard_map/ppermute | solution.py:866
  9.0 4.7 %collective-permute-start = (bf16[512,768]{1,0:T(8,128)(2,1)S(1)}, bf16[512,768]{1,0:T(8,128)(2,1)}, u32[]{:S(2)}, u32[]{:S(2)}) collective-permute-start(bf16[512,768]{1,0:T(8,128)(2,1)S(1)} %dynamic-slice_bitcast_fusion.1), channel_id=1, source_target_pairs={{0,1},{1,0},{2,3},{3,2},{4,5},{5,4},{6,7},{7,6},{8,9},{9,8},{10,11... | collective-permute-start | bytes 2359304 | tf_op jit(solution)/shard_map/ppermute | solution.py:866
  10.1 3.4 collective-permute-start.3
  10.6 15.9 %collective-permute-start.5 = (bf16[2,6]{1,0:T(2,128)(2,1)S(1)}, bf16[2,6]{1,0:T(2,128)(2,1)S(1)}, u32[]{:S(2)}, u32[]{:S(2)}) collective-permute-start(bf16[2,6]{1,0:T(2,128)(2,1)S(1)} %copy-done.37), channel_id=1, source_target_pairs={{0,1},{1,0},{2,3},{3,2},{4,5},{5,4},{6,7},{7,6},{8,9},{9,8},{10,11... | collective-permute-start | bytes 80 | tf_op jit(solution)/shard_map/ppermute | solution.py:866
  10.7 1.9 collective-permute-start.2
  12.6 14.0 %collective-permute-start.6 = (bf16[1536]{0:T(1024)(128)(2,1)S(1)}, bf16[1536]{0:T(1024)(128)(2,1)S(1)}, u32[]{:S(2)}, u32[]{:S(2)}) collective-permute-start(bf16[1536]{0:T(1024)(128)(2,1)S(1)} %copy-done.35), channel_id=1, source_target_pairs={{0,1},{1,0},{2,3},{3,2},{4,5},{5,4},{6,7},{7,6},{8,9},{9,8},{10,11... | collective-permute-start | bytes 9224 | tf_op jit(solution)/shard_map/ppermute | solution.py:866
  13.5 13.0 %copy-start.38 = (bf16[768,1536]{1,0:T(8,128)(2,1)S(1)}, bf16[768,1536]{1,0:T(8,128)(2,1)}, u32[]{:S(2)}) copy-start(bf16[768,1536]{1,0:T(8,128)(2,1)} %refs_10_.1) | copy-start | bytes 7077892
  13.5 16.1 %copy-start.43 = (bf16[384,768]{1,0:T(8,128)(2,1)S(1)}, bf16[384,768]{1,0:T(8,128)(2,1)}, u32[]{:S(2)}) copy-start(bf16[384,768]{1,0:T(8,128)(2,1)} %refs_4_.1) | copy-start | bytes 1769476
  13.6 16.4 %copy-start.14 = (bf16[2,512,768]{2,1,0:T(8,128)(2,1)S(1)}, bf16[2,512,768]{2,1,0:T(8,128)(2,1)}, u32[]{:S(2)}) copy-start(bf16[2,512,768]{2,1,0:T(8,128)(2,1)} %refs_6_.1) | copy-start | bytes 4718596
  13.6 13.0 %collective-permute-start.4 = (bf16[2,6,256]{2,0,1:T(2,128)(2,1)S(1)}, bf16[2,6,256]{2,0,1:T(2,128)(2,1)S(1)}, u32[]{:S(2)}, u32[]{:S(2)}) collective-permute-start(bf16[2,6,256]{2,0,1:T(2,128)(2,1)S(1)} %copy-done.28), channel_id=1, source_target_pairs={{0,1},{1,0},{2,3},{3,2},{4,5},{5,4},{6,7},{7,6},{8,9},{9,8},{10,11... | collective-permute-start | bytes 18440 | tf_op jit(solution)/shard_map/ppermute | solution.py:866
  26.6 22.4 %collective-permute-start.9 = (bf16[768,1536]{1,0:T(8,128)(2,1)S(1)}, bf16[768,1536]{1,0:T(8,128)(2,1)S(1)}, u32[]{:S(2)}, u32[]{:S(2)}) collective-permute-start(bf16[768,1536]{1,0:T(8,128)(2,1)S(1)} %copy-done.38), channel_id=1, source_target_pairs={{0,1},{1,0},{2,3},{3,2},{4,5},{5,4},{6,7},{7,6},{8,9},{9,8},{10,11... | collective-permute-start | bytes 7077896 | tf_op jit(solution)/shard_map/ppermute | solution.py:866
  27.0 22.0 %collective-permute-start.10 = (bf16[1536,768]{1,0:T(8,128)(2,1)}, bf16[1536,768]{1,0:T(8,128)(2,1)}, u32[]{:S(2)}, u32[]{:S(2)}) collective-permute-start(bf16[1536,768]{1,0:T(8,128)(2,1)} %refs_14_.1), channel_id=1, source_target_pairs={{0,1},{1,0},{2,3},{3,2},{4,5},{5,4},{6,7},{7,6},{8,9},{9,8},{10,11... | collective-permute-start | bytes 7077896 | tf_op jit(solution)/shard_map/ppermute | solution.py:866
  29.6 19.3 %collective-permute-start.7 = (bf16[384,768]{1,0:T(8,128)(2,1)S(1)}, bf16[384,768]{1,0:T(8,128)(2,1)}, u32[]{:S(2)}, u32[]{:S(2)}) collective-permute-start(bf16[384,768]{1,0:T(8,128)(2,1)S(1)} %copy-done.43), channel_id=1, source_target_pairs={{0,1},{1,0},{2,3},{3,2},{4,5},{5,4},{6,7},{7,6},{8,9},{9,8},{10,11... | collective-permute-start | bytes 1769480 | tf_op jit(solution)/shard_map/ppermute | solution.py:866
  30.0 18.9 %collective-permute-start.8 = (bf16[512,768]{1,0:T(8,128)(2,1)S(1)}, bf16[512,768]{1,0:T(8,128)(2,1)S(1)}, u32[]{:S(2)}, u32[]{:S(2)}) collective-permute-start(bf16[512,768]{1,0:T(8,128)(2,1)S(1)} %dynamic-slice_bitcast_fusion), channel_id=1, source_target_pairs={{0,1},{1,0},{2,3},{3,2},{4,5},{5,4},{6,7},{7,6},{8,9},{9,8},{10,11... | collective-permute-start | bytes 2359304 | tf_op jit(solution)/shard_map/ppermute | solution.py:866
  49.0 1.6 copy-start.39
  116.2 23.2 %collective-permute-start.12 = (bf16[768,1536]{1,0:T(8,128)(2,1)}, bf16[768,1536]{1,0:T(8,128)(2,1)S(1)}, u32[]{:S(2)}, u32[]{:S(2)}) collective-permute-start(bf16[768,1536]{1,0:T(8,128)(2,1)} %get-tuple-element.114), channel_id=1, source_target_pairs={{0,1},{1,0},{2,3},{3,2},{4,5},{5,4},{6,7},{7,6},{8,9},{9,8},{10,11... | collective-permute-start | bytes 7077896 | tf_op jit(solution)/shard_map/ppermute | solution.py:866
  116.6 22.7 %collective-permute-start.13 = (bf16[1536,768]{1,0:T(8,128)(2,1)}, bf16[1536,768]{1,0:T(8,128)(2,1)S(1)}, u32[]{:S(2)}, u32[]{:S(2)}) collective-permute-start(bf16[1536,768]{1,0:T(8,128)(2,1)} %get-tuple-element.116), channel_id=1, source_target_pairs={{0,1},{1,0},{2,3},{3,2},{4,5},{5,4},{6,7},{7,6},{8,9},{9,8},{10,11... | collective-permute-start | bytes 7077896 | tf_op jit(solution)/shard_map/ppermute | solution.py:866
  116.7 22.4 %copy-start.44 = (bf16[768,384]{1,0:T(8,128)(2,1)S(1)}, bf16[768,384]{1,0:T(8,128)(2,1)}, u32[]{:S(2)}) copy-start(bf16[768,384]{1,0:T(8,128)(2,1)} %get-tuple-element.139) | copy-start | bytes 1769476
  138.8 29.8 %collective-permute-start.14 = (bf16[2304,384]{1,0:T(8,128)(2,1)}, bf16[2304,384]{1,0:T(8,128)(2,1)}, u32[]{:S(2)}, u32[]{:S(2)}) collective-permute-start(bf16[2304,384]{1,0:T(8,128)(2,1)} %get-tuple-element.137), channel_id=1, source_target_pairs={{0,1},{1,0},{2,3},{3,2},{4,5},{5,4},{6,7},{7,6},{8,9},{9,8},{10,11... | collective-permute-start | bytes 5308424 | tf_op jit(solution)/shard_map/ppermute | solution.py:866
  139.2 29.3 %collective-permute-start.15 = (bf16[768,384]{1,0:T(8,128)(2,1)S(1)}, bf16[768,384]{1,0:T(8,128)(2,1)S(1)}, u32[]{:S(2)}, u32[]{:S(2)}) collective-permute-start(bf16[768,384]{1,0:T(8,128)(2,1)S(1)} %copy-done.44), channel_id=1, source_target_pairs={{0,1},{1,0},{2,3},{3,2},{4,5},{5,4},{6,7},{7,6},{8,9},{9,8},{10,11... | collective-permute-start | bytes 1769480 | tf_op jit(solution)/shard_map/ppermute | solution.py:866
  139.3 1.4 copy-start
  139.3 2.2 copy-start.3
  169.4 11.2 %copy-start.40 = (bf16[512,768]{1,0:T(8,128)(2,1)S(1)}, bf16[512,768]{1,0:T(8,128)(2,1)}, u32[]{:S(2)}) copy-start(bf16[512,768]{1,0:T(8,128)(2,1)} %get-tuple-element.109) | copy-start | bytes 2359300
  176.2 27.8 %collective-permute-start.16 = (bf16[1152,384]{1,0:T(8,128)(2,1)}, bf16[1152,384]{1,0:T(8,128)(2,1)S(1)}, u32[]{:S(2)}, u32[]{:S(2)}) collective-permute-start(bf16[1152,384]{1,0:T(8,128)(2,1)} %get-tuple-element.146), channel_id=1, source_target_pairs={{0,2},{2,0},{4,6},{6,4},{8,10},{10,8},{12,14},{14,12},{16,18},{18,... | collective-permute-start | bytes 2654216 | tf_op jit(solution)/shard_map/ppermute | solution.py:870
  179.0 26.4 %collective-permute-start.17 = (bf16[1152,384]{1,0:T(8,128)(2,1)}, bf16[1152,384]{1,0:T(8,128)(2,1)S(1)}, u32[]{:S(2)}, u32[]{:S(2)}) collective-permute-start(bf16[1152,384]{1,0:T(8,128)(2,1)} %get-tuple-element.140.refs_16_), channel_id=1, source_target_pairs={{0,4},{2,6},{4,0},{6,2},{8,12},{10,14},{12,8},{14,10},{16,20},{18,... | collective-permute-start | bytes 2654216 | tf_op jit(solution)/shard_map/ppermute | solution.py:870
  180.6 33.2 %collective-permute-start.11 = (bf16[512,768]{1,0:T(8,128)(2,1)S(1)}, bf16[512,768]{1,0:T(8,128)(2,1)S(1)}, u32[]{:S(2)}, u32[]{:S(2)}) collective-permute-start(bf16[512,768]{1,0:T(8,128)(2,1)S(1)} %copy-done.40), channel_id=1, source_target_pairs={{0,1},{1,0},{2,3},{3,2},{4,5},{5,4},{6,7},{7,6},{8,9},{9,8},{10,11... | collective-permute-start | bytes 2359304 | tf_op jit(solution)/shard_map/ppermute | solution.py:866
  204.0 1.5 copy-start.1
  206.4 5.2 %copy-start.41 = (bf16[512,768]{1,0:T(8,128)(2,1)S(1)}, bf16[512,768]{1,0:T(8,128)(2,1)}, u32[]{:S(2)}) copy-start(bf16[512,768]{1,0:T(8,128)(2,1)} %get-tuple-element.149) | copy-start | bytes 2359300
  206.4 7.4 %copy-start.45 = (bf16[128,768]{1,0:T(8,128)(2,1)S(1)}, bf16[128,768]{1,0:T(8,128)(2,1)}, u32[]{:S(2)}) copy-start(bf16[128,768]{1,0:T(8,128)(2,1)} %get-tuple-element.150) | copy-start | bytes 589828
  211.5 3.7 %collective-permute-start.18 = (bf16[512,768]{1,0:T(8,128)(2,1)S(1)}, bf16[512,768]{1,0:T(8,128)(2,1)S(1)}, u32[]{:S(2)}, u32[]{:S(2)}) collective-permute-start(bf16[512,768]{1,0:T(8,128)(2,1)S(1)} %copy-done.41), channel_id=1, source_target_pairs={{0,1},{1,0},{2,3},{3,2},{4,5},{5,4},{6,7},{7,6},{8,9},{9,8},{10,11... | collective-permute-start | bytes 2359304 | tf_op jit(solution)/shard_map/ppermute | solution.py:866
  211.6 15.3 %collective-permute-start.21 = (bf16[576,384]{1,0:T(8,128)(2,1)}, bf16[576,384]{1,0:T(8,128)(2,1)S(1)}, u32[]{:S(2)}, u32[]{:S(2)}) collective-permute-start(bf16[576,384]{1,0:T(8,128)(2,1)} %get-tuple-element.160), channel_id=1, source_target_pairs={{0,4},{2,6},{4,0},{6,2},{8,12},{10,14},{12,8},{14,10},{16,20},{18,... | collective-permute-start | bytes 1327112 | tf_op jit(solution)/shard_map/ppermute | solution.py:870
  213.2 13.7 %collective-permute-start.22 = (bf16[576,384]{1,0:T(8,128)(2,1)}, bf16[576,384]{1,0:T(8,128)(2,1)S(1)}, u32[]{:S(2)}, u32[]{:S(2)}) collective-permute-start(bf16[576,384]{1,0:T(8,128)(2,1)} %get-tuple-element.154.refs_7_), channel_id=1, source_target_pairs={{0,2},{2,0},{4,6},{6,4},{8,10},{10,8},{12,14},{14,12},{16,18},{18,... | collective-permute-start | bytes 1327112 | tf_op jit(solution)/shard_map/ppermute | solution.py:870
  213.8 1.4 collective-permute-start.19
  213.8 1.4 copy-start.8
  220.0 15.3 %copy-start.22 = (f32[96,128]{1,0:T(8,128)S(1)}, f32[96,128]{1,0:T(8,128)}, u32[]{:S(2)}) copy-start(f32[96,128]{1,0:T(8,128)} %get-tuple-element.159.refs_9_) | copy-start | bytes 147460
  230.9 14.4 %collective-permute-start.25 = (bf16[288,384]{1,0:T(8,128)(2,1)}, bf16[288,384]{1,0:T(8,128)(2,1)S(1)}, u32[]{:S(2)}, u32[]{:S(2)}) collective-permute-start(bf16[288,384]{1,0:T(8,128)(2,1)} %get-tuple-element.164), channel_id=1, source_target_pairs={{0,8},{2,10},{4,12},{6,14},{8,0},{10,2},{12,4},{14,6},{16,24},{18,... | collective-permute-start | bytes 663560 | tf_op jit(solution)/shard_map/ppermute | solution.py:870
  232.4 21.3 %collective-permute-start.26 = (bf16[288,384]{1,0:T(8,128)(2,1)}, bf16[288,384]{1,0:T(8,128)(2,1)S(1)}, u32[]{:S(2)}, u32[]{:S(2)}) collective-permute-start(bf16[288,384]{1,0:T(8,128)(2,1)} %get-tuple-element.165), channel_id=1, source_target_pairs={{0,16},{2,18},{4,20},{6,22},{8,24},{10,26},{12,28},{14,30},{16,0},... | collective-permute-start | bytes 663560 | tf_op jit(solution)/shard_map/ppermute | solution.py:870
  235.0 18.7 %collective-permute-start.27 = (bf16[288,384]{1,0:T(8,128)(2,1)}, bf16[288,384]{1,0:T(8,128)(2,1)S(1)}, u32[]{:S(2)}, u32[]{:S(2)}) collective-permute-start(bf16[288,384]{1,0:T(8,128)(2,1)} %get-tuple-element.162.refs_2_), channel_id=1, source_target_pairs={{0,24},{2,26},{4,28},{6,30},{8,16},{10,18},{12,20},{14,22},{16,8},... | collective-permute-start | bytes 663560 | tf_op jit(solution)/shard_map/ppermute | solution.py:870
  235.3 1.2 collective-permute-start.20
  238.6 4.6 %collective-permute-start.23 = (f32[96,128]{1,0:T(8,128)}, f32[96,128]{1,0:T(8,128)S(1)}, u32[]{:S(2)}, u32[]{:S(2)}) collective-permute-start(f32[96,128]{1,0:T(8,128)} %small_add.5.refs_0_.refs_2_), channel_id=1, source_target_pairs={{0,2},{2,0},{4,6},{6,4},{8,10},{10,8},{12,14},{14,12},{16,18},{18,... | collective-permute-start | bytes 147464 | tf_op jit(solution)/shard_map/ppermute | solution.py:870
  245.3 8.4 %copy-start.15 = (bf16[288,384]{1,0:T(8,128)(2,1)}, bf16[288,384]{1,0:T(8,128)(2,1)S(1)}, u32[]{:S(2)}) copy-start(bf16[288,384]{1,0:T(8,128)(2,1)S(1)} %collective-permute-done.25.refs_1_) | copy-start | bytes 663556
  256.5 16.1 %collective-permute-start.31 = (bf16[288,384]{1,0:T(8,128)(2,1)}, bf16[288,384]{1,0:T(8,128)(2,1)S(1)}, u32[]{:S(2)}, u32[]{:S(2)}) collective-permute-start(bf16[288,384]{1,0:T(8,128)(2,1)} %total.1.refs_2_.refs_1_), channel_id=1, source_target_pairs={{0,24},{2,26},{4,28},{6,30},{8,16},{10,18},{12,20},{14,22},{16,8},... | collective-permute-start | bytes 663560 | tf_op jit(solution)/shard_map/ppermute | solution.py:870
  258.9 26.9 %collective-permute-start.30 = (bf16[288,384]{1,0:T(8,128)(2,1)}, bf16[288,384]{1,0:T(8,128)(2,1)S(1)}, u32[]{:S(2)}, u32[]{:S(2)}) collective-permute-start(bf16[288,384]{1,0:T(8,128)(2,1)} %total.1.refs_2_.refs_1_), channel_id=1, source_target_pairs={{0,16},{2,18},{4,20},{6,22},{8,24},{10,26},{12,28},{14,30},{16,0},... | collective-permute-start | bytes 663560 | tf_op jit(solution)/shard_map/ppermute | solution.py:870
  265.4 20.5 %collective-permute-start.29 = (bf16[288,384]{1,0:T(8,128)(2,1)}, bf16[288,384]{1,0:T(8,128)(2,1)S(1)}, u32[]{:S(2)}, u32[]{:S(2)}) collective-permute-start(bf16[288,384]{1,0:T(8,128)(2,1)} %total.1.refs_2_.refs_1_), channel_id=1, source_target_pairs={{0,8},{2,10},{4,12},{6,14},{8,0},{10,2},{12,4},{14,6},{16,24},{18,... | collective-permute-start | bytes 663560 | tf_op jit(solution)/shard_map/ppermute | solution.py:870
  265.4 5.1 %collective-permute-start.24 = (f32[96,128]{1,0:T(8,128)}, f32[96,128]{1,0:T(8,128)S(1)}, u32[]{:S(2)}, u32[]{:S(2)}) collective-permute-start(f32[96,128]{1,0:T(8,128)} %small_add.6.refs_4_.refs_0_), channel_id=1, source_target_pairs={{0,4},{2,6},{4,0},{6,2},{8,12},{10,14},{12,8},{14,10},{16,20},{18,... | collective-permute-start | bytes 147464 | tf_op jit(solution)/shard_map/ppermute | solution.py:870
  272.6 21.1 %copy-start.11 = (f32[96,128]{1,0:T(8,128)S(1)}, f32[96,128]{1,0:T(8,128)}, u32[]{:S(2)}) copy-start(f32[96,128]{1,0:T(8,128)} %small_add.7.refs_5_.refs_0_) | copy-start | bytes 147460
  272.6 13.3 %copy-start.18 = (bf16[288,384]{1,0:T(8,128)(2,1)}, bf16[288,384]{1,0:T(8,128)(2,1)S(1)}, u32[]{:S(2)}) copy-start(bf16[288,384]{1,0:T(8,128)(2,1)S(1)} %collective-permute-done.31.refs_4_) | copy-start | bytes 663556
  290.2 32.2 %collective-permute-start.35 = (bf16[1152,384]{1,0:T(8,128)(2,1)}, bf16[1152,384]{1,0:T(8,128)(2,1)S(1)}, u32[]{:S(2)}, u32[]{:S(2)}) collective-permute-start(bf16[1152,384]{1,0:T(8,128)(2,1)} %spread.1.refs_2_.refs_1_), channel_id=1, source_target_pairs={{0,6},{2,4},{4,2},{6,0},{8,14},{10,12},{12,10},{14,8},{16,22},{18,... | collective-permute-start | bytes 2654216 | tf_op jit(solution)/shard_map/ppermute | solution.py:870
  291.6 48.7 %collective-permute-start.34 = (bf16[1152,384]{1,0:T(8,128)(2,1)}, bf16[1152,384]{1,0:T(8,128)(2,1)S(1)}, u32[]{:S(2)}, u32[]{:S(2)}) collective-permute-start(bf16[1152,384]{1,0:T(8,128)(2,1)} %spread.1.refs_2_.refs_1_), channel_id=1, source_target_pairs={{0,4},{2,6},{4,0},{6,2},{8,12},{10,14},{12,8},{14,10},{16,20},{18,... | collective-permute-start | bytes 2654216 | tf_op jit(solution)/shard_map/ppermute | solution.py:870
  292.1 48.2 %collective-permute-start.33 = (bf16[1152,384]{1,0:T(8,128)(2,1)}, bf16[1152,384]{1,0:T(8,128)(2,1)S(1)}, u32[]{:S(2)}, u32[]{:S(2)}) collective-permute-start(bf16[1152,384]{1,0:T(8,128)(2,1)} %spread.1.refs_2_.refs_1_), channel_id=1, source_target_pairs={{0,2},{2,0},{4,6},{6,4},{8,10},{10,8},{12,14},{14,12},{16,18},{18,... | collective-permute-start | bytes 2654216 | tf_op jit(solution)/shard_map/ppermute | solution.py:870
  293.7 7.5 %collective-permute-start.28 = (f32[96,128]{1,0:T(8,128)S(1)}, f32[96,128]{1,0:T(8,128)S(1)}, u32[]{:S(2)}, u32[]{:S(2)}) collective-permute-start(f32[96,128]{1,0:T(8,128)S(1)} %copy-done.11), channel_id=1, source_target_pairs={{0,8},{2,10},{4,12},{6,14},{8,0},{10,2},{12,4},{14,6},{16,24},{18,... | collective-permute-start | bytes 147464 | tf_op jit(solution)/shard_map/ppermute | solution.py:870
  303.3 7.2 %collective-permute-start.32 = (f32[96,128]{1,0:T(8,128)}, f32[96,128]{1,0:T(8,128)S(1)}, u32[]{:S(2)}, u32[]{:S(2)}) collective-permute-start(f32[96,128]{1,0:T(8,128)} %small_add.8.refs_0_.refs_2_), channel_id=1, source_target_pairs={{0,16},{2,18},{4,20},{6,22},{8,24},{10,26},{12,28},{14,30},{16,0},... | collective-permute-start | bytes 147464 | tf_op jit(solution)/shard_map/ppermute | solution.py:870
  322.4 17.9 %copy-start.5 = (bf16[1152,384]{1,0:T(8,128)(2,1)}, bf16[1152,384]{1,0:T(8,128)(2,1)S(1)}, u32[]{:S(2)}) copy-start(bf16[1152,384]{1,0:T(8,128)(2,1)S(1)} %collective-permute-done.35.refs_4_) | copy-start | bytes 2654212
  (19 other events, 14.9 us)
Sparse Core Ops, SparseCore 0:
  146.8 197.6 all-reduce.2
where the time goes:
time: 362 us; the launch traced here: 361 us
  Pallas kernels  202 us (56%)
  waiting for transfers between devices  85.5 us (24%)
  starting transfers between devices  29.7 us (8%)
  local copies, waits for them, and re-layouts  26.5 us (7%)
  between operations  14.7 us (4%)
    pallas_call x21, Pallas kernels, call(): pl.pallas_call(body, grid_spec=pltpu.PrefetchScalarGridSpec(num_scalar_pr...  202 us
    ppermute x17, waiting for transfers between devices, across(): lax.ppermute(values, 'batch', [(i, i ^ offset) for i in range(count)])  82.8 us
    ppermute x17, starting transfers between devices, across(): lax.ppermute(values, 'batch', [(i, i ^ offset) for i in range(count)])  25.1 us
    unnamed x93, local copies, waits for them, and re-layouts  16.4 us
  transfers between devices with their start and end apart: 37, of which 14 were waited for; matrix products, arithmetic and copies ran while one was open for 4% of the time, Pallas kernels for 36%

commit v1 on v0

--- a/solution.py
+++ b/solution.py
@@ -577,8 +577,9 @@
 
             @pl.when((step >= steps) == (side == 1))
             def _():
-                for held, source in zip((up, ub, down), weights):
-                    held[...] = source[...]
+                up[...] = weights[0][...]
+                ub[...] = weights[1][side : side + 1, :]
+                down[...] = weights[2][...]
 
         forward, backward = feed_step(normed, normed_t, out_grad, up, ub, down, du, dub, dd)
         out_sum[...] += forward
@@ -654,8 +655,8 @@
             once(vectors.shape),
             up_spec(far_block),
             up_spec(own_block),
-            bias_spec(far_block, 1),
-            bias_spec(own_block, 1),
+            bias_spec(far_block, 2),
+            bias_spec(own_block, 2),
             down_spec(far_block),
             down_spec(own_block),
         ],
@@ -981,7 +982,7 @@
         )
 
     def cuts(self, rows):
-        return 4 if rows % 64 == 0 else 1
+        return 2 if rows % 32 == 0 else 1
 
     def first(self, quads):
         self.halve(0, quads)
@@ -1290,6 +1291,7 @@
     vectors = jnp.stack(
         [first_gain, first_bias, out_bias, second_gain, second_bias, down_bias] + [down_bias] * 2
     )
+    up_biases = jnp.stack([ub_far, up_bias_vector]).astype(F32)
     order = Order()
     hid, norm_t, q, k, v, mem_k, mem_v, coeffs_t = project(
         order, scalars, hidden_in, hidden_come, vectors, w_own, w_far, query_bias, memory_coeffs, coeffs_come
@@ -1331,8 +1333,8 @@
         vectors,
         up_far,
         up_matrix,
-        ub_far.astype(F32)[None],
-        up_bias_vector.astype(F32)[None],
+        up_biases,
+        up_biases,
         down_far,
         down_matrix,
     )

time: 362 us -> 360 us (level)
  transfers between devices with their start and end apart: 37 -> 37, of which waited for: 14 -> 14; matrix products, arithmetic and copies ran while one was open for 4% -> 3% of each run, Pallas kernels for 36% -> 36%
where the time goes in v1:
time: 360 us; the launch traced here: 359 us
  Pallas kernels  201 us (56%)
  waiting for transfers between devices  85.4 us (24%)
  starting transfers between devices  29.9 us (8%)
  local copies, waits for them, and re-layouts  25.3 us (7%)
  between operations  14.7 us (4%)
    pallas_call x21, Pallas kernels, call(): pl.pallas_call(body, grid_spec=pltpu.PrefetchScalarGridSpec(num_scalar_pr...  201 us
    ppermute x17, waiting for transfers between devices, across(): lax.ppermute(values, 'batch', [(i, i ^ offset) for i in range(count)])  82.7 us
    ppermute x17, starting transfers between devices, across(): lax.ppermute(values, 'batch', [(i, i ^ offset) for i in range(count)])  25.3 us
    unnamed x93, local copies, waits for them, and re-layouts  16.4 us
  transfers between devices with their start and end apart: 37, of which 14 were waited for; matrix products, arithmetic and copies ran while one was open for 3% of the time, Pallas kernels for 36%

profile of v1, /device:TPU:0, one launch (start us, length us, event | category | flops | bytes accessed | tf_op | source)
XLA Modules:
  0.0 359.1 jit_solution(1017452014996059098)
XLA Ops:
  7.9 1.2 dynamic-slice_bitcast_fusion.1
  9.2 0.9 dynamic-slice_bitcast_fusion.2
  13.8 1.2 copy-done.4
  15.0 11.5 %project.1 = (bf16[1024,768]{1,0:T(8,128)(2,1)}, bf16[768,1024]{1,0:T(8,128)(2,1)}, bf16[1024,768]{1,0:T(8,128)(2,1)}, bf16[1024,768]{1,0:T(8,128)(2,1)}, bf16[1...) custom-call(s32[7]{0:T(128)} %stack.63.refs_0_, ...), custom_call_target="tpu_custom_call" | custom-call | flops 3623878656 | bytes 18087936 | tf_op jit(solution)/shard_map/project/pallas_call | solution.py:88
  29.7 18.7 %attend.1 = (f32[768,1024]{1,0:T(8,128)}, bf16[768,1024]{1,0:T(8,128)(2,1)}, bf16[1024,768]{1,0:T(8,128)(2,1)}, f32[48,1024]{1,0:T(8,128)}) custom-call(s32[7]{0:T(128)} %stack.63.refs_0_, s32[2]{0:T(128)} %refs_1_.7, bf16[1024,768]{1,0:T(8,128)(2,1)} %get-tuple-element.95.refs_2_, bf16[1024,768]{1,0:T(8,128)(2,1)} %get-tuple-element.96.refs_3_, ...), custom_call_target="tpu_custom_call" | custom-call | flops 9663676416 | bytes 12976128 | tf_op jit(solution)/shard_map/attend/pallas_call | solution.py:88
  48.4 0.8 copy-done.42
  49.3 0.8 copy-done.39
  50.1 65.6 %feed.1 = (bf16[768,1536]{1,0:T(8,128)(2,1)}, bf16[768,1536]{1,0:T(8,128)(2,1)}, f32[8,1536]{1,0:T(8,128)}, f32[8,1536]{1,0:T(8,128)}, bf16[1536,768]{1,0:T(8,12...) custom-call(s32[7]{0:T(128)} %stack.63.refs_0_, ...), custom_call_target="tpu_custom_call" | custom-call | flops 28991029248 | bytes 35635200 | tf_op jit(solution)/shard_map/feed/pallas_call | solution.py:88
  116.2 22.0 %attend_back.2 = (bf16[1024,384]{1,0:T(8,128)(2,1)}, bf16[1024,384]{1,0:T(8,128)(2,1)}, bf16[1024,384]{1,0:T(8,128)(2,1)}, bf16[256,384]{1,0:T(8,128)(2,1)}, bf1...) custom-call(s32[7]{0:T(128)} %stack.63.refs_0_, s32[2]{0:T(128)} %refs_1_.7, ...), custom_call_target="tpu_custom_call" | custom-call | flops 13086228480 | bytes 9142272 | tf_op jit(solution)/shard_map/attend_back/pallas_call | solution.py:88
  138.8 1.4 copy-done
  140.2 0.8 copy-done.3
  141.0 5.2 %peers_added.1 = (bf16[768,768]{1,0:T(8,128)(2,1)}, bf16[1536,768]{1,0:T(8,128)(2,1)}, f32[8,128]{1,0:T(8,128)}) custom-call(bf16[768,1536]{1,0:T(8,128)(2,1)} %get-tuple-element.113.refs_0_.refs_2_.refs_6_.refs_10_.refs_14_, bf16[768,1536]{1,0:T(8,128)(2,1)} %copy-done, bf16[1536,768]{1,0:T(8,128)(2,1)} %get-tuple-element.115.refs_2_, ...), custom_call_target="tpu_custom_call" | custom-call | bytes 7086080 | tf_op jit(solution)/shard_map/peers_added/pallas_call | solution.py:88
  146.2 21.8 %attend_back.3 = (bf16[1024,384]{1,0:T(8,128)(2,1)}, bf16[1024,384]{1,0:T(8,128)(2,1)}, bf16[1024,384]{1,0:T(8,128)(2,1)}, bf16[256,384]{1,0:T(8,128)(2,1)}, bf1...) custom-call(s32[7]{0:T(128)} %stack.63.refs_0_, s32[2]{0:T(128)} %refs_1_.7, ...), custom_call_target="tpu_custom_call" | custom-call | flops 13086228480 | bytes 9142272 | tf_op jit(solution)/shard_map/attend_back/pallas_call | solution.py:88
  168.0 0.8 copy-done.10
  168.8 6.9 %mixed_halve.1 = (bf16[1152,384]{1,0:T(8,128)(2,1)}, bf16[1152,384]{1,0:T(8,128)(2,1)}, bf16[1152,384]{1,0:T(8,128)(2,1)}, bf16[1152,384]{1,0:T(8,128)(2,1)}) custom-call(s32[7]{0:T(128)} %stack.63.refs_0_, bf16[2304,384]{1,0:T(8,128)(2,1)} %get-tuple-element.136.refs_1_.refs_5_.refs_9_, ...), custom_call_target="tpu_custom_call" | custom-call | bytes 7077888 | tf_op jit(solution)/shard_map/mixed_halve/pallas_call | solution.py:88
  175.7 2.8 collective-permute-start.16
  178.5 1.5 collective-permute-start.17
  180.0 13.3 %input_back.1 = (f32[2,512,768]{2,1,0:T(8,128)}, bf16[512,768]{1,0:T(8,128)(2,1)}, f32[2,128,768]{2,1,0:T(8,128)}, bf16[128,768]{1,0:T(8,128)(2,1)}, f32[8,768]{1,0:T(8,128)}) custom-call(s32[7]{0:T(128)} %stack.63.refs_0_, bf16[1024,768]{1,0:T(8,128)(2,1)} %get-tuple-element.102.refs_2_.refs_1_, f32[1024,768]{1,0:T(8,128)} %get-tuple-element.125.refs_2_, ...), custom_call_target="tpu_custom_call" | custom-call | flops 3623878656 | bytes 9879552 | tf_op jit(solution)/shard_map/input_back/pallas_call | solution.py:88
  193.3 1.6 pack.1
  194.9 8.5 %collective-permute-done.16.refs_3_.refs_4_ = bf16[1152,384]{1,0:T(8,128)(2,1)S(1)} collective-permute-done((bf16[1152,384]{1,0:T(8,128)(2,1)}, bf16[1152,384]{1,0:T(8,128)(2,1)S(1)}, u32[]{:S(2)}, u32[]{:S(2)}) %collective-permute-start.16) | collective-permute-done | bytes 884768 | tf_op jit(solution)/shard_map/ppermute | solution.py:871
  203.5 1.5 collective-permute-done.17.refs_7_.refs_8_
  204.9 0.9 copy-done.2
  205.9 4.1 %halve.1 = (bf16[576,384]{1,0:T(8,128)(2,1)}, bf16[576,384]{1,0:T(8,128)(2,1)}, bf16[576,384]{1,0:T(8,128)(2,1)}, bf16[576,384]{1,0:T(8,128)(2,1)}) custom-call(s32[7]{0:T(128)} %stack.63.refs_0_, bf16[1152,384]{1,0:T(8,128)(2,1)} %get-tuple-element.145.refs_1_.refs_2_, bf16[1152,384]{1,0:T(8,128)(2,1)} %get-tuple-element.145.refs_1_.refs_2_, ...), custom_call_target="tpu_custom_call" | custom-call | bytes 3538944 | tf_op jit(solution)/shard_map/halve/pallas_call | solution.py:88
  210.1 1.6 collective-permute-start.21
  212.3 1.4 collective-permute-done.19.refs_3_
  214.6 3.7 %tokens_place.1 = (bf16[2,512,768]{2,1,0:T(8,128)(2,1)}, f32[2,512,768]{2,1,0:T(8,128)}, f32[2,128,768]{2,1,0:T(8,128)}) custom-call(s32[7]{0:T(128)} %stack.63.refs_0_, bf16[512,768]{1,0:T(8,128)(2,1)} %copy-done.8, bf16[512,768]{1,0:T(8,128)(2,1)} %copy-done.9, ...), custom_call_target="tpu_custom_call", output_to_operand_aliasing={{0}: (4, {}), {1}: (5, {}), {2}: (6, {})} | custom-call | bytes 11010048 | tf_op jit(solution)/shard_map/tokens_place/pallas_call | solution.py:88
  218.3 7.0 %collective-permute-done.21.refs_2_ = bf16[576,384]{1,0:T(8,128)(2,1)S(1)} collective-permute-done((bf16[576,384]{1,0:T(8,128)(2,1)}, bf16[576,384]{1,0:T(8,128)(2,1)S(1)}, u32[]{:S(2)}, u32[]{:S(2)}) %collective-permute-start.21) | collective-permute-done | bytes 442400 | tf_op jit(solution)/shard_map/ppermute | solution.py:871
  225.3 0.8 copy-done.12
  226.2 3.1 share.1
  229.4 1.5 collective-permute-start.25
  230.9 2.6 collective-permute-start.26
  233.7 1.2 collective-permute-done.20.refs_1_
  235.6 1.4 small_add.5.refs_0_.refs_2_
  237.7 4.1 %collective-permute-done.23.refs_1_ = f32[96,128]{1,0:T(8,128)S(1)} collective-permute-done((f32[96,128]{1,0:T(8,128)}, f32[96,128]{1,0:T(8,128)S(1)}, u32[]{:S(2)}, u32[]{:S(2)}) %collective-permute-start.23) | collective-permute-done | bytes 49184 | tf_op jit(solution)/shard_map/ppermute | solution.py:871
  242.4 1.4 small_add.6.refs_4_.refs_0_
  243.8 8.3 %collective-permute-done.26.refs_2_ = bf16[288,384]{1,0:T(8,128)(2,1)S(1)} collective-permute-done((bf16[288,384]{1,0:T(8,128)(2,1)}, bf16[288,384]{1,0:T(8,128)(2,1)S(1)}, u32[]{:S(2)}, u32[]{:S(2)}) %collective-permute-start.26) | collective-permute-done | bytes 221216 | tf_op jit(solution)/shard_map/ppermute | solution.py:871
  252.2 0.7 copy-done.16
  252.9 2.1 total.1.refs_2_.refs_1_
  255.0 2.4 collective-permute-start.31
  257.4 6.4 %collective-permute-start.30 = (bf16[288,384]{1,0:T(8,128)(2,1)}, bf16[288,384]{1,0:T(8,128)(2,1)S(1)}, u32[]{:S(2)}, u32[]{:S(2)}) collective-permute-start(bf16[288,384]{1,0:T(8,128)(2,1)} %total.1.refs_2_.refs_1_), channel_id=1, source_target_pairs={{0,16},{2,18},{4,20},{6,22},{8,24},{10,26},{12,28},{14,30},{16,0},... | collective-permute-start | bytes 663560 | tf_op jit(solution)/shard_map/ppermute | solution.py:871
  263.9 1.3 collective-permute-start.24
  265.3 3.8 %collective-permute-done.24.refs_1_ = f32[96,128]{1,0:T(8,128)S(1)} collective-permute-done((f32[96,128]{1,0:T(8,128)}, f32[96,128]{1,0:T(8,128)S(1)}, u32[]{:S(2)}, u32[]{:S(2)}) %collective-permute-start.24) | collective-permute-done | bytes 49184 | tf_op jit(solution)/shard_map/ppermute | solution.py:871
  269.7 1.4 small_add.7.refs_5_.refs_0_
  271.2 13.1 %collective-permute-done.30.refs_3_ = bf16[288,384]{1,0:T(8,128)(2,1)S(1)} collective-permute-done((bf16[288,384]{1,0:T(8,128)(2,1)}, bf16[288,384]{1,0:T(8,128)(2,1)S(1)}, u32[]{:S(2)}, u32[]{:S(2)}) %collective-permute-start.30) | collective-permute-done | bytes 221216 | tf_op jit(solution)/shard_map/ppermute | solution.py:871
  284.3 0.7 copy-done.19
  285.0 0.7 copy-done.20
  285.7 3.0 spread.1.refs_2_.refs_1_
  288.6 1.4 collective-permute-start.35
  290.0 0.7 collective-permute-start.34
  290.7 1.4 collective-permute-start.33
  292.1 7.6 %collective-permute-done.28.refs_1_ = f32[96,128]{1,0:T(8,128)S(1)} collective-permute-done((f32[96,128]{1,0:T(8,128)S(1)}, f32[96,128]{1,0:T(8,128)S(1)}, u32[]{:S(2)}, u32[]{:S(2)}) %collective-permute-start.28) | collective-permute-done | bytes 49184 | tf_op jit(solution)/shard_map/ppermute | solution.py:871
  300.4 1.4 small_add.8.refs_0_.refs_2_
  301.8 7.2 %collective-permute-done.32.refs_1_ = f32[96,128]{1,0:T(8,128)S(1)} collective-permute-done((f32[96,128]{1,0:T(8,128)}, f32[96,128]{1,0:T(8,128)S(1)}, u32[]{:S(2)}, u32[]{:S(2)}) %collective-permute-start.32) | collective-permute-done | bytes 49184 | tf_op jit(solution)/shard_map/ppermute | solution.py:871
  309.6 1.4 small_add.9.refs_5_
  311.0 0.7 slice.45
  311.7 0.8 slice_reduce_fusion
  313.9 1.4 slice_bitcast_fusion.1
  315.9 1.3 slice_bitcast_fusion
  317.2 3.6 %collective-permute-done.35.refs_4_ = bf16[1152,384]{1,0:T(8,128)(2,1)S(1)} collective-permute-done((bf16[1152,384]{1,0:T(8,128)(2,1)}, bf16[1152,384]{1,0:T(8,128)(2,1)S(1)}, u32[]{:S(2)}, u32[]{:S(2)}) %collective-permute-start.35) | collective-permute-done | bytes 884768 | tf_op jit(solution)/shard_map/ppermute | solution.py:871
  320.8 17.9 %collective-permute-done.34.refs_3_ = bf16[1152,384]{1,0:T(8,128)(2,1)S(1)} collective-permute-done((bf16[1152,384]{1,0:T(8,128)(2,1)}, bf16[1152,384]{1,0:T(8,128)(2,1)S(1)}, u32[]{:S(2)}, u32[]{:S(2)}) %collective-permute-start.34) | collective-permute-done | bytes 884768 | tf_op jit(solution)/shard_map/ppermute | solution.py:871
  338.7 0.9 copy-done.6
  339.6 0.9 copy-done.7
  340.6 6.2 %mixed_place.1 = (f32[2304,384]{1,0:T(8,128)}, f32[768,1536]{1,0:T(8,128)}, f32[384,768]{1,0:T(8,128)}) custom-call(s32[7]{0:T(128)} %stack.63.refs_0_, bf16[1152,384]{1,0:T(8,128)(2,1)} %spread.1.refs_2_.refs_1_, bf16[1152,384]{1,0:T(8,128)(2,1)} %copy-done.7, bf16[1152,384]{1,0:T(8,128)(2,1)} %copy-done.6, bf16[1152,384]{1,0:T(8,128)(2,1)} %copy-done.5, ...), custom_call_target="tpu_custom_call" | custom-call | bytes 18874368 | tf_op jit(solution)/shard_map/mixed_place/pallas_call | solution.py:88
  346.7 5.3 %feed_place.1 = (f32[768,1536]{1,0:T(8,128)}, f32[1536,768]{1,0:T(8,128)}) custom-call(bf16[768,768]{1,0:T(8,128)(2,1)} %get-tuple-element.207.refs_0_, bf16[1536,768]{1,0:T(8,128)(2,1)} %get-tuple-element.208.refs_1_, f32[768,1536]{1,0:T(8,128)} %get-tuple-element.170.refs_2_, f32[384,768]{1,0:T(8,128)} %get-tuple-element.199.refs_3_), custom_call_target="tpu_custom_call", output_to_operand_aliasing={{0}: (2, {})} | custom-call | bytes 18874368 | tf_op jit(solution)/shard_map/feed_place/pallas_call | solution.py:88
  (149 shorter events, 16.5 us)
Async XLA Ops:
  7.2 3.4 copy-start.37
  7.2 3.5 copy-start.36
  7.2 3.9 %copy-start.29 = (f32[768]{0:T(1024)S(1)}, f32[768]{0:T(1024)}, u32[]{:S(2)}) copy-start(f32[768]{0:T(1024)} %param.21) | copy-start | bytes 9220
  7.2 3.9 %copy-start.30 = (f32[768]{0:T(1024)S(1)}, f32[768]{0:T(1024)}, u32[]{:S(2)}) copy-start(f32[768]{0:T(1024)} %param.22) | copy-start | bytes 9220
  7.2 3.9 %copy-start.31 = (f32[768]{0:T(1024)S(1)}, f32[768]{0:T(1024)}, u32[]{:S(2)}) copy-start(f32[768]{0:T(1024)} %param.28) | copy-start | bytes 9220
  7.2 3.9 %copy-start.32 = (f32[768]{0:T(1024)S(1)}, f32[768]{0:T(1024)}, u32[]{:S(2)}) copy-start(f32[768]{0:T(1024)} %param.29) | copy-start | bytes 9220
  7.3 4.0 %copy-start.33 = (f32[768]{0:T(1024)S(1)}, f32[768]{0:T(1024)}, u32[]{:S(2)}) copy-start(f32[768]{0:T(1024)} %param.30) | copy-start | bytes 9220
  7.3 4.0 %copy-start.34 = (f32[768]{0:T(1024)S(1)}, f32[768]{0:T(1024)}, u32[]{:S(2)}) copy-start(f32[768]{0:T(1024)} %param.34) | copy-start | bytes 9220
  7.3 5.3 %copy-start.35 = (bf16[1536]{0:T(1024)(128)(2,1)S(1)}, bf16[1536]{0:T(1024)(128)(2,1)}, u32[]{:S(2)}) copy-start(bf16[1536]{0:T(1024)(128)(2,1)} %param.32) | copy-start | bytes 9220
  7.3 6.3 %copy-start.28 = (bf16[2,6,256]{2,0,1:T(2,128)(2,1)S(1)}, bf16[2,6,256]{2,0,1:T(2,128)(2,1)}, u32[]{:S(2)}) copy-start(bf16[2,6,256]{2,0,1:T(2,128)(2,1)} %param.25) | copy-start | bytes 18436
  7.3 339.4 %all-reduce.3.cloned.1.call-start = ((), (), s32[]{:S(2)}) async-start(), calls=%async_computation | async-start | bytes 7077888 | tf_op jit(solution)/shard_map/psum | solution.py:1350
  7.3 6.5 %collective-permute-start.1 = (bf16[3,768,384]{2,1,0:T(8,128)(2,1)}, bf16[3,768,384]{2,1,0:T(8,128)(2,1)S(1)}, u32[]{:S(2)}, u32[]{:S(2)}) collective-permute-start(bf16[3,768,384]{2,1,0:T(8,128)(2,1)} %bitcast.35), channel_id=1, source_target_pairs={{0,1},{1,0},{2,3},{3,2},{4,5},{5,4},{6,7},{7,6},{8,9},{9,8},{10,11... | collective-permute-start | bytes 5308424 | tf_op jit(solution)/shard_map/ppermute | solution.py:867
  9.0 4.7 %collective-permute-start = (bf16[512,768]{1,0:T(8,128)(2,1)S(1)}, bf16[512,768]{1,0:T(8,128)(2,1)}, u32[]{:S(2)}, u32[]{:S(2)}) collective-permute-start(bf16[512,768]{1,0:T(8,128)(2,1)S(1)} %dynamic-slice_bitcast_fusion.1), channel_id=1, source_target_pairs={{0,1},{1,0},{2,3},{3,2},{4,5},{5,4},{6,7},{7,6},{8,9},{9,8},{10,11... | collective-permute-start | bytes 2359304 | tf_op jit(solution)/shard_map/ppermute | solution.py:867
  10.1 3.4 collective-permute-start.3
  10.6 15.9 %collective-permute-start.5 = (bf16[2,6]{1,0:T(2,128)(2,1)S(1)}, bf16[2,6]{1,0:T(2,128)(2,1)S(1)}, u32[]{:S(2)}, u32[]{:S(2)}) collective-permute-start(bf16[2,6]{1,0:T(2,128)(2,1)S(1)} %copy-done.37), channel_id=1, source_target_pairs={{0,1},{1,0},{2,3},{3,2},{4,5},{5,4},{6,7},{7,6},{8,9},{9,8},{10,11... | collective-permute-start | bytes 80 | tf_op jit(solution)/shard_map/ppermute | solution.py:867
  10.7 1.9 collective-permute-start.2
  12.6 14.0 %collective-permute-start.6 = (bf16[1536]{0:T(1024)(128)(2,1)S(1)}, bf16[1536]{0:T(1024)(128)(2,1)S(1)}, u32[]{:S(2)}, u32[]{:S(2)}) collective-permute-start(bf16[1536]{0:T(1024)(128)(2,1)S(1)} %copy-done.35), channel_id=1, source_target_pairs={{0,1},{1,0},{2,3},{3,2},{4,5},{5,4},{6,7},{7,6},{8,9},{9,8},{10,11... | collective-permute-start | bytes 9224 | tf_op jit(solution)/shard_map/ppermute | solution.py:867
  13.5 13.0 %copy-start.38 = (bf16[768,1536]{1,0:T(8,128)(2,1)S(1)}, bf16[768,1536]{1,0:T(8,128)(2,1)}, u32[]{:S(2)}) copy-start(bf16[768,1536]{1,0:T(8,128)(2,1)} %refs_10_.1) | copy-start | bytes 7077892
  13.5 15.5 %copy-start.43 = (bf16[384,768]{1,0:T(8,128)(2,1)S(1)}, bf16[384,768]{1,0:T(8,128)(2,1)}, u32[]{:S(2)}) copy-start(bf16[384,768]{1,0:T(8,128)(2,1)} %refs_4_.1) | copy-start | bytes 1769476
  13.5 15.9 %copy-start.14 = (bf16[2,512,768]{2,1,0:T(8,128)(2,1)S(1)}, bf16[2,512,768]{2,1,0:T(8,128)(2,1)}, u32[]{:S(2)}) copy-start(bf16[2,512,768]{2,1,0:T(8,128)(2,1)} %refs_6_.1) | copy-start | bytes 4718596
  13.6 13.0 %collective-permute-start.4 = (bf16[2,6,256]{2,0,1:T(2,128)(2,1)S(1)}, bf16[2,6,256]{2,0,1:T(2,128)(2,1)S(1)}, u32[]{:S(2)}, u32[]{:S(2)}) collective-permute-start(bf16[2,6,256]{2,0,1:T(2,128)(2,1)S(1)} %copy-done.28), channel_id=1, source_target_pairs={{0,1},{1,0},{2,3},{3,2},{4,5},{5,4},{6,7},{7,6},{8,9},{9,8},{10,11... | collective-permute-start | bytes 18440 | tf_op jit(solution)/shard_map/ppermute | solution.py:867
  26.6 21.8 %collective-permute-start.9 = (bf16[768,1536]{1,0:T(8,128)(2,1)S(1)}, bf16[768,1536]{1,0:T(8,128)(2,1)S(1)}, u32[]{:S(2)}, u32[]{:S(2)}) collective-permute-start(bf16[768,1536]{1,0:T(8,128)(2,1)S(1)} %copy-done.38), channel_id=1, source_target_pairs={{0,1},{1,0},{2,3},{3,2},{4,5},{5,4},{6,7},{7,6},{8,9},{9,8},{10,11... | collective-permute-start | bytes 7077896 | tf_op jit(solution)/shard_map/ppermute | solution.py:867
  27.0 21.4 %collective-permute-start.10 = (bf16[1536,768]{1,0:T(8,128)(2,1)}, bf16[1536,768]{1,0:T(8,128)(2,1)}, u32[]{:S(2)}, u32[]{:S(2)}) collective-permute-start(bf16[1536,768]{1,0:T(8,128)(2,1)} %refs_14_.1), channel_id=1, source_target_pairs={{0,1},{1,0},{2,3},{3,2},{4,5},{5,4},{6,7},{7,6},{8,9},{9,8},{10,11... | collective-permute-start | bytes 7077896 | tf_op jit(solution)/shard_map/ppermute | solution.py:867
  29.1 19.3 %collective-permute-start.7 = (bf16[384,768]{1,0:T(8,128)(2,1)S(1)}, bf16[384,768]{1,0:T(8,128)(2,1)}, u32[]{:S(2)}, u32[]{:S(2)}) collective-permute-start(bf16[384,768]{1,0:T(8,128)(2,1)S(1)} %copy-done.43), channel_id=1, source_target_pairs={{0,1},{1,0},{2,3},{3,2},{4,5},{5,4},{6,7},{7,6},{8,9},{9,8},{10,11... | collective-permute-start | bytes 1769480 | tf_op jit(solution)/shard_map/ppermute | solution.py:867
  29.5 18.9 %collective-permute-start.8 = (bf16[512,768]{1,0:T(8,128)(2,1)S(1)}, bf16[512,768]{1,0:T(8,128)(2,1)S(1)}, u32[]{:S(2)}, u32[]{:S(2)}) collective-permute-start(bf16[512,768]{1,0:T(8,128)(2,1)S(1)} %dynamic-slice_bitcast_fusion), channel_id=1, source_target_pairs={{0,1},{1,0},{2,3},{3,2},{4,5},{5,4},{6,7},{7,6},{8,9},{9,8},{10,11... | collective-permute-start | bytes 2359304 | tf_op jit(solution)/shard_map/ppermute | solution.py:867
  48.4 1.6 copy-start.39
  115.6 23.2 %collective-permute-start.12 = (bf16[768,1536]{1,0:T(8,128)(2,1)}, bf16[768,1536]{1,0:T(8,128)(2,1)S(1)}, u32[]{:S(2)}, u32[]{:S(2)}) collective-permute-start(bf16[768,1536]{1,0:T(8,128)(2,1)} %get-tuple-element.114), channel_id=1, source_target_pairs={{0,1},{1,0},{2,3},{3,2},{4,5},{5,4},{6,7},{7,6},{8,9},{9,8},{10,11... | collective-permute-start | bytes 7077896 | tf_op jit(solution)/shard_map/ppermute | solution.py:867
  116.1 22.7 %collective-permute-start.13 = (bf16[1536,768]{1,0:T(8,128)(2,1)}, bf16[1536,768]{1,0:T(8,128)(2,1)S(1)}, u32[]{:S(2)}, u32[]{:S(2)}) collective-permute-start(bf16[1536,768]{1,0:T(8,128)(2,1)} %get-tuple-element.116), channel_id=1, source_target_pairs={{0,1},{1,0},{2,3},{3,2},{4,5},{5,4},{6,7},{7,6},{8,9},{9,8},{10,11... | collective-permute-start | bytes 7077896 | tf_op jit(solution)/shard_map/ppermute | solution.py:867
  116.2 22.4 %copy-start.44 = (bf16[768,384]{1,0:T(8,128)(2,1)S(1)}, bf16[768,384]{1,0:T(8,128)(2,1)}, u32[]{:S(2)}) copy-start(bf16[768,384]{1,0:T(8,128)(2,1)} %get-tuple-element.139) | copy-start | bytes 1769476
  138.2 29.8 %collective-permute-start.14 = (bf16[2304,384]{1,0:T(8,128)(2,1)}, bf16[2304,384]{1,0:T(8,128)(2,1)}, u32[]{:S(2)}, u32[]{:S(2)}) collective-permute-start(bf16[2304,384]{1,0:T(8,128)(2,1)} %get-tuple-element.137), channel_id=1, source_target_pairs={{0,1},{1,0},{2,3},{3,2},{4,5},{5,4},{6,7},{7,6},{8,9},{9,8},{10,11... | collective-permute-start | bytes 5308424 | tf_op jit(solution)/shard_map/ppermute | solution.py:867
  138.7 29.3 %collective-permute-start.15 = (bf16[768,384]{1,0:T(8,128)(2,1)S(1)}, bf16[768,384]{1,0:T(8,128)(2,1)S(1)}, u32[]{:S(2)}, u32[]{:S(2)}) collective-permute-start(bf16[768,384]{1,0:T(8,128)(2,1)S(1)} %copy-done.44), channel_id=1, source_target_pairs={{0,1},{1,0},{2,3},{3,2},{4,5},{5,4},{6,7},{7,6},{8,9},{9,8},{10,11... | collective-permute-start | bytes 1769480 | tf_op jit(solution)/shard_map/ppermute | solution.py:867
  138.8 1.4 copy-start
  138.8 2.2 copy-start.3
  168.8 11.2 %copy-start.40 = (bf16[512,768]{1,0:T(8,128)(2,1)S(1)}, bf16[512,768]{1,0:T(8,128)(2,1)}, u32[]{:S(2)}) copy-start(bf16[512,768]{1,0:T(8,128)(2,1)} %get-tuple-element.109) | copy-start | bytes 2359300
  175.7 27.8 %collective-permute-start.16 = (bf16[1152,384]{1,0:T(8,128)(2,1)}, bf16[1152,384]{1,0:T(8,128)(2,1)S(1)}, u32[]{:S(2)}, u32[]{:S(2)}) collective-permute-start(bf16[1152,384]{1,0:T(8,128)(2,1)} %get-tuple-element.146), channel_id=1, source_target_pairs={{0,2},{2,0},{4,6},{6,4},{8,10},{10,8},{12,14},{14,12},{16,18},{18,... | collective-permute-start | bytes 2654216 | tf_op jit(solution)/shard_map/ppermute | solution.py:871
  178.5 26.4 %collective-permute-start.17 = (bf16[1152,384]{1,0:T(8,128)(2,1)}, bf16[1152,384]{1,0:T(8,128)(2,1)S(1)}, u32[]{:S(2)}, u32[]{:S(2)}) collective-permute-start(bf16[1152,384]{1,0:T(8,128)(2,1)} %get-tuple-element.140.refs_16_), channel_id=1, source_target_pairs={{0,4},{2,6},{4,0},{6,2},{8,12},{10,14},{12,8},{14,10},{16,20},{18,... | collective-permute-start | bytes 2654216 | tf_op jit(solution)/shard_map/ppermute | solution.py:871
  180.0 32.2 %collective-permute-start.11 = (bf16[512,768]{1,0:T(8,128)(2,1)S(1)}, bf16[512,768]{1,0:T(8,128)(2,1)S(1)}, u32[]{:S(2)}, u32[]{:S(2)}) collective-permute-start(bf16[512,768]{1,0:T(8,128)(2,1)S(1)} %copy-done.40), channel_id=1, source_target_pairs={{0,1},{1,0},{2,3},{3,2},{4,5},{5,4},{6,7},{7,6},{8,9},{9,8},{10,11... | collective-permute-start | bytes 2359304 | tf_op jit(solution)/shard_map/ppermute | solution.py:867
  203.5 1.5 copy-start.1
  205.9 4.1 %copy-start.41 = (bf16[512,768]{1,0:T(8,128)(2,1)S(1)}, bf16[512,768]{1,0:T(8,128)(2,1)}, u32[]{:S(2)}) copy-start(bf16[512,768]{1,0:T(8,128)(2,1)} %get-tuple-element.149) | copy-start | bytes 2359300
  205.9 6.4 %copy-start.45 = (bf16[128,768]{1,0:T(8,128)(2,1)S(1)}, bf16[128,768]{1,0:T(8,128)(2,1)}, u32[]{:S(2)}) copy-start(bf16[128,768]{1,0:T(8,128)(2,1)} %get-tuple-element.150) | copy-start | bytes 589828
  210.0 3.7 %collective-permute-start.18 = (bf16[512,768]{1,0:T(8,128)(2,1)S(1)}, bf16[512,768]{1,0:T(8,128)(2,1)S(1)}, u32[]{:S(2)}, u32[]{:S(2)}) collective-permute-start(bf16[512,768]{1,0:T(8,128)(2,1)S(1)} %copy-done.41), channel_id=1, source_target_pairs={{0,1},{1,0},{2,3},{3,2},{4,5},{5,4},{6,7},{7,6},{8,9},{9,8},{10,11... | collective-permute-start | bytes 2359304 | tf_op jit(solution)/shard_map/ppermute | solution.py:867
  210.1 15.3 %collective-permute-start.21 = (bf16[576,384]{1,0:T(8,128)(2,1)}, bf16[576,384]{1,0:T(8,128)(2,1)S(1)}, u32[]{:S(2)}, u32[]{:S(2)}) collective-permute-start(bf16[576,384]{1,0:T(8,128)(2,1)} %get-tuple-element.160), channel_id=1, source_target_pairs={{0,4},{2,6},{4,0},{6,2},{8,12},{10,14},{12,8},{14,10},{16,20},{18,... | collective-permute-start | bytes 1327112 | tf_op jit(solution)/shard_map/ppermute | solution.py:871
  211.7 13.7 %collective-permute-start.22 = (bf16[576,384]{1,0:T(8,128)(2,1)}, bf16[576,384]{1,0:T(8,128)(2,1)S(1)}, u32[]{:S(2)}, u32[]{:S(2)}) collective-permute-start(bf16[576,384]{1,0:T(8,128)(2,1)} %get-tuple-element.154.refs_7_), channel_id=1, source_target_pairs={{0,2},{2,0},{4,6},{6,4},{8,10},{10,8},{12,14},{14,12},{16,18},{18,... | collective-permute-start | bytes 1327112 | tf_op jit(solution)/shard_map/ppermute | solution.py:871
  212.2 1.4 collective-permute-start.19
  212.2 1.4 copy-start.8
  218.3 15.4 %copy-start.22 = (f32[96,128]{1,0:T(8,128)S(1)}, f32[96,128]{1,0:T(8,128)}, u32[]{:S(2)}) copy-start(f32[96,128]{1,0:T(8,128)} %get-tuple-element.159.refs_9_) | copy-start | bytes 147460
  229.4 14.5 %collective-permute-start.25 = (bf16[288,384]{1,0:T(8,128)(2,1)}, bf16[288,384]{1,0:T(8,128)(2,1)S(1)}, u32[]{:S(2)}, u32[]{:S(2)}) collective-permute-start(bf16[288,384]{1,0:T(8,128)(2,1)} %get-tuple-element.164), channel_id=1, source_target_pairs={{0,8},{2,10},{4,12},{6,14},{8,0},{10,2},{12,4},{14,6},{16,24},{18,... | collective-permute-start | bytes 663560 | tf_op jit(solution)/shard_map/ppermute | solution.py:871
  230.9 21.3 %collective-permute-start.26 = (bf16[288,384]{1,0:T(8,128)(2,1)}, bf16[288,384]{1,0:T(8,128)(2,1)S(1)}, u32[]{:S(2)}, u32[]{:S(2)}) collective-permute-start(bf16[288,384]{1,0:T(8,128)(2,1)} %get-tuple-element.165), channel_id=1, source_target_pairs={{0,16},{2,18},{4,20},{6,22},{8,24},{10,26},{12,28},{14,30},{16,0},... | collective-permute-start | bytes 663560 | tf_op jit(solution)/shard_map/ppermute | solution.py:871
  233.5 18.6 %collective-permute-start.27 = (bf16[288,384]{1,0:T(8,128)(2,1)}, bf16[288,384]{1,0:T(8,128)(2,1)S(1)}, u32[]{:S(2)}, u32[]{:S(2)}) collective-permute-start(bf16[288,384]{1,0:T(8,128)(2,1)} %get-tuple-element.162.refs_2_), channel_id=1, source_target_pairs={{0,24},{2,26},{4,28},{6,30},{8,16},{10,18},{12,20},{14,22},{16,8},... | collective-permute-start | bytes 663560 | tf_op jit(solution)/shard_map/ppermute | solution.py:871
  233.7 1.2 collective-permute-start.20
  237.0 4.7 %collective-permute-start.23 = (f32[96,128]{1,0:T(8,128)}, f32[96,128]{1,0:T(8,128)S(1)}, u32[]{:S(2)}, u32[]{:S(2)}) collective-permute-start(f32[96,128]{1,0:T(8,128)} %small_add.5.refs_0_.refs_2_), channel_id=1, source_target_pairs={{0,2},{2,0},{4,6},{6,4},{8,10},{10,8},{12,14},{14,12},{16,18},{18,... | collective-permute-start | bytes 147464 | tf_op jit(solution)/shard_map/ppermute | solution.py:871
  243.8 8.3 %copy-start.15 = (bf16[288,384]{1,0:T(8,128)(2,1)}, bf16[288,384]{1,0:T(8,128)(2,1)S(1)}, u32[]{:S(2)}) copy-start(bf16[288,384]{1,0:T(8,128)(2,1)S(1)} %collective-permute-done.25.refs_1_) | copy-start | bytes 663556
  255.0 16.2 %collective-permute-start.31 = (bf16[288,384]{1,0:T(8,128)(2,1)}, bf16[288,384]{1,0:T(8,128)(2,1)S(1)}, u32[]{:S(2)}, u32[]{:S(2)}) collective-permute-start(bf16[288,384]{1,0:T(8,128)(2,1)} %total.1.refs_2_.refs_1_), channel_id=1, source_target_pairs={{0,24},{2,26},{4,28},{6,30},{8,16},{10,18},{12,20},{14,22},{16,8},... | collective-permute-start | bytes 663560 | tf_op jit(solution)/shard_map/ppermute | solution.py:871
  257.4 26.9 %collective-permute-start.30 = (bf16[288,384]{1,0:T(8,128)(2,1)}, bf16[288,384]{1,0:T(8,128)(2,1)S(1)}, u32[]{:S(2)}, u32[]{:S(2)}) collective-permute-start(bf16[288,384]{1,0:T(8,128)(2,1)} %total.1.refs_2_.refs_1_), channel_id=1, source_target_pairs={{0,16},{2,18},{4,20},{6,22},{8,24},{10,26},{12,28},{14,30},{16,0},... | collective-permute-start | bytes 663560 | tf_op jit(solution)/shard_map/ppermute | solution.py:871
  263.8 20.5 %collective-permute-start.29 = (bf16[288,384]{1,0:T(8,128)(2,1)}, bf16[288,384]{1,0:T(8,128)(2,1)S(1)}, u32[]{:S(2)}, u32[]{:S(2)}) collective-permute-start(bf16[288,384]{1,0:T(8,128)(2,1)} %total.1.refs_2_.refs_1_), channel_id=1, source_target_pairs={{0,8},{2,10},{4,12},{6,14},{8,0},{10,2},{12,4},{14,6},{16,24},{18,... | collective-permute-start | bytes 663560 | tf_op jit(solution)/shard_map/ppermute | solution.py:871
  263.9 5.2 %collective-permute-start.24 = (f32[96,128]{1,0:T(8,128)}, f32[96,128]{1,0:T(8,128)S(1)}, u32[]{:S(2)}, u32[]{:S(2)}) collective-permute-start(f32[96,128]{1,0:T(8,128)} %small_add.6.refs_4_.refs_0_), channel_id=1, source_target_pairs={{0,4},{2,6},{4,0},{6,2},{8,12},{10,14},{12,8},{14,10},{16,20},{18,... | collective-permute-start | bytes 147464 | tf_op jit(solution)/shard_map/ppermute | solution.py:871
  271.1 21.0 %copy-start.11 = (f32[96,128]{1,0:T(8,128)S(1)}, f32[96,128]{1,0:T(8,128)}, u32[]{:S(2)}) copy-start(f32[96,128]{1,0:T(8,128)} %small_add.7.refs_5_.refs_0_) | copy-start | bytes 147460
  271.1 13.1 %copy-start.18 = (bf16[288,384]{1,0:T(8,128)(2,1)}, bf16[288,384]{1,0:T(8,128)(2,1)S(1)}, u32[]{:S(2)}) copy-start(bf16[288,384]{1,0:T(8,128)(2,1)S(1)} %collective-permute-done.31.refs_4_) | copy-start | bytes 663556
  288.6 32.2 %collective-permute-start.35 = (bf16[1152,384]{1,0:T(8,128)(2,1)}, bf16[1152,384]{1,0:T(8,128)(2,1)S(1)}, u32[]{:S(2)}, u32[]{:S(2)}) collective-permute-start(bf16[1152,384]{1,0:T(8,128)(2,1)} %spread.1.refs_2_.refs_1_), channel_id=1, source_target_pairs={{0,6},{2,4},{4,2},{6,0},{8,14},{10,12},{12,10},{14,8},{16,22},{18,... | collective-permute-start | bytes 2654216 | tf_op jit(solution)/shard_map/ppermute | solution.py:871
  290.0 48.7 %collective-permute-start.34 = (bf16[1152,384]{1,0:T(8,128)(2,1)}, bf16[1152,384]{1,0:T(8,128)(2,1)S(1)}, u32[]{:S(2)}, u32[]{:S(2)}) collective-permute-start(bf16[1152,384]{1,0:T(8,128)(2,1)} %spread.1.refs_2_.refs_1_), channel_id=1, source_target_pairs={{0,4},{2,6},{4,0},{6,2},{8,12},{10,14},{12,8},{14,10},{16,20},{18,... | collective-permute-start | bytes 2654216 | tf_op jit(solution)/shard_map/ppermute | solution.py:871
  290.7 48.0 %collective-permute-start.33 = (bf16[1152,384]{1,0:T(8,128)(2,1)}, bf16[1152,384]{1,0:T(8,128)(2,1)S(1)}, u32[]{:S(2)}, u32[]{:S(2)}) collective-permute-start(bf16[1152,384]{1,0:T(8,128)(2,1)} %spread.1.refs_2_.refs_1_), channel_id=1, source_target_pairs={{0,2},{2,0},{4,6},{6,4},{8,10},{10,8},{12,14},{14,12},{16,18},{18,... | collective-permute-start | bytes 2654216 | tf_op jit(solution)/shard_map/ppermute | solution.py:871
  292.1 7.6 %collective-permute-start.28 = (f32[96,128]{1,0:T(8,128)S(1)}, f32[96,128]{1,0:T(8,128)S(1)}, u32[]{:S(2)}, u32[]{:S(2)}) collective-permute-start(f32[96,128]{1,0:T(8,128)S(1)} %copy-done.11), channel_id=1, source_target_pairs={{0,8},{2,10},{4,12},{6,14},{8,0},{10,2},{12,4},{14,6},{16,24},{18,... | collective-permute-start | bytes 147464 | tf_op jit(solution)/shard_map/ppermute | solution.py:871
  301.8 7.2 %collective-permute-start.32 = (f32[96,128]{1,0:T(8,128)}, f32[96,128]{1,0:T(8,128)S(1)}, u32[]{:S(2)}, u32[]{:S(2)}) collective-permute-start(f32[96,128]{1,0:T(8,128)} %small_add.8.refs_0_.refs_2_), channel_id=1, source_target_pairs={{0,16},{2,18},{4,20},{6,22},{8,24},{10,26},{12,28},{14,30},{16,0},... | collective-permute-start | bytes 147464 | tf_op jit(solution)/shard_map/ppermute | solution.py:871
  320.8 17.9 %copy-start.5 = (bf16[1152,384]{1,0:T(8,128)(2,1)}, bf16[1152,384]{1,0:T(8,128)(2,1)S(1)}, u32[]{:S(2)}) copy-start(bf16[1152,384]{1,0:T(8,128)(2,1)S(1)} %collective-permute-done.35.refs_4_) | copy-start | bytes 2654212
  (19 other events, 14.9 us)
Sparse Core Ops, SparseCore 0:
  146.3 197.3 all-reduce.2

commit v2 on v1

--- a/solution.py
+++ b/solution.py
@@ -982,7 +982,7 @@
         )
 
     def cuts(self, rows):
-        return 2 if rows % 32 == 0 else 1
+        return 1
 
     def first(self, quads):
         self.halve(0, quads)
@@ -1063,7 +1063,7 @@
 
 
 def peers_added(order, up_pair, down_pair):
-    cuts = 4
+    cuts = 2
     width = down_pair[0].shape[1]
     up_spec = pl.BlockSpec((up_pair[0].shape[0] // cuts, width), lambda i: (i, 1))
     up_out = pl.BlockSpec((up_pair[0].shape[0] // cuts, width), lambda i: (i, 0))

time: 360 us -> 359 us (level)
  no operation moved by 1% of the time
where the time goes in v2:
time: 359 us
  Pallas kernels  201 us (56%)
  waiting for transfers between devices  85.4 us (24%)
  starting transfers between devices  29.8 us (8%)
  local copies, waits for them, and re-layouts  25.3 us (7%)
  between operations  14.7 us (4%)
    pallas_call x21, Pallas kernels, call(): pl.pallas_call(body, grid_spec=pltpu.PrefetchScalarGridSpec(num_scalar_pr...  201 us
    ppermute x17, waiting for transfers between devices, across(): lax.ppermute(values, 'batch', [(i, i ^ offset) for i in range(count)])  82.7 us
    ppermute x17, starting transfers between devices, across(): lax.ppermute(values, 'batch', [(i, i ^ offset) for i in range(count)])  25.2 us
    unnamed x93, local copies, waits for them, and re-layouts  16.4 us
  transfers between devices with their start and end apart: 37, of which 14 were waited for; matrix products, arithmetic and copies ran while one was open for 3% of the time, Pallas kernels for 36%

profile of v2, /device:TPU:0, one launch (start us, length us, event | category | flops | bytes accessed | tf_op | source)
XLA Modules:
  0.0 358.7 jit_solution(9727588408674650915)
XLA Ops:
  7.9 1.2 dynamic-slice_bitcast_fusion.1
  9.2 0.9 dynamic-slice_bitcast_fusion.2
  13.8 1.2 copy-done.4
  15.0 11.5 %project.1 = (bf16[1024,768]{1,0:T(8,128)(2,1)}, bf16[768,1024]{1,0:T(8,128)(2,1)}, bf16[1024,768]{1,0:T(8,128)(2,1)}, bf16[1024,768]{1,0:T(8,128)(2,1)}, bf16[1...) custom-call(s32[7]{0:T(128)} %stack.63.refs_0_, ...), custom_call_target="tpu_custom_call" | custom-call | flops 3623878656 | bytes 18087936 | tf_op jit(solution)/shard_map/project/pallas_call | solution.py:88
  29.7 18.7 %attend.1 = (f32[768,1024]{1,0:T(8,128)}, bf16[768,1024]{1,0:T(8,128)(2,1)}, bf16[1024,768]{1,0:T(8,128)(2,1)}, f32[48,1024]{1,0:T(8,128)}) custom-call(s32[7]{0:T(128)} %stack.63.refs_0_, s32[2]{0:T(128)} %refs_1_.7, bf16[1024,768]{1,0:T(8,128)(2,1)} %get-tuple-element.95.refs_2_, bf16[1024,768]{1,0:T(8,128)(2,1)} %get-tuple-element.96.refs_3_, ...), custom_call_target="tpu_custom_call" | custom-call | flops 9663676416 | bytes 12976128 | tf_op jit(solution)/shard_map/attend/pallas_call | solution.py:88
  48.4 0.8 copy-done.42
  49.3 0.8 copy-done.39
  50.1 65.7 %feed.1 = (bf16[768,1536]{1,0:T(8,128)(2,1)}, bf16[768,1536]{1,0:T(8,128)(2,1)}, f32[8,1536]{1,0:T(8,128)}, f32[8,1536]{1,0:T(8,128)}, bf16[1536,768]{1,0:T(8,12...) custom-call(s32[7]{0:T(128)} %stack.63.refs_0_, ...), custom_call_target="tpu_custom_call" | custom-call | flops 28991029248 | bytes 35635200 | tf_op jit(solution)/shard_map/feed/pallas_call | solution.py:88
  116.4 22.0 %attend_back.2 = (bf16[1024,384]{1,0:T(8,128)(2,1)}, bf16[1024,384]{1,0:T(8,128)(2,1)}, bf16[1024,384]{1,0:T(8,128)(2,1)}, bf16[256,384]{1,0:T(8,128)(2,1)}, bf1...) custom-call(s32[7]{0:T(128)} %stack.63.refs_0_, s32[2]{0:T(128)} %refs_1_.7, ...), custom_call_target="tpu_custom_call" | custom-call | flops 13086228480 | bytes 9142272 | tf_op jit(solution)/shard_map/attend_back/pallas_call | solution.py:88
  139.0 1.4 copy-done
  140.4 0.8 copy-done.3
  141.2 4.5 %peers_added.1 = (bf16[768,768]{1,0:T(8,128)(2,1)}, bf16[1536,768]{1,0:T(8,128)(2,1)}, f32[8,128]{1,0:T(8,128)}) custom-call(bf16[768,1536]{1,0:T(8,128)(2,1)} %get-tuple-element.113.refs_0_.refs_2_.refs_6_.refs_10_.refs_14_, bf16[768,1536]{1,0:T(8,128)(2,1)} %copy-done, bf16[1536,768]{1,0:T(8,128)(2,1)} %get-tuple-element.115.refs_2_, ...), custom_call_target="tpu_custom_call" | custom-call | bytes 7086080 | tf_op jit(solution)/shard_map/peers_added/pallas_call | solution.py:88
  145.6 21.8 %attend_back.3 = (bf16[1024,384]{1,0:T(8,128)(2,1)}, bf16[1024,384]{1,0:T(8,128)(2,1)}, bf16[1024,384]{1,0:T(8,128)(2,1)}, bf16[256,384]{1,0:T(8,128)(2,1)}, bf1...) custom-call(s32[7]{0:T(128)} %stack.63.refs_0_, s32[2]{0:T(128)} %refs_1_.7, ...), custom_call_target="tpu_custom_call" | custom-call | flops 13086228480 | bytes 9142272 | tf_op jit(solution)/shard_map/attend_back/pallas_call | solution.py:88
  167.5 0.8 copy-done.10
  168.3 6.9 %mixed_halve.1 = (bf16[1152,384]{1,0:T(8,128)(2,1)}, bf16[1152,384]{1,0:T(8,128)(2,1)}, bf16[1152,384]{1,0:T(8,128)(2,1)}, bf16[1152,384]{1,0:T(8,128)(2,1)}) custom-call(s32[7]{0:T(128)} %stack.63.refs_0_, bf16[2304,384]{1,0:T(8,128)(2,1)} %get-tuple-element.136.refs_1_.refs_5_.refs_9_, ...), custom_call_target="tpu_custom_call" | custom-call | bytes 7077888 | tf_op jit(solution)/shard_map/mixed_halve/pallas_call | solution.py:88
  175.2 2.8 collective-permute-start.16
  178.0 1.5 collective-permute-start.17
  179.5 13.3 %input_back.1 = (f32[2,512,768]{2,1,0:T(8,128)}, bf16[512,768]{1,0:T(8,128)(2,1)}, f32[2,128,768]{2,1,0:T(8,128)}, bf16[128,768]{1,0:T(8,128)(2,1)}, f32[8,768]{1,0:T(8,128)}) custom-call(s32[7]{0:T(128)} %stack.63.refs_0_, bf16[1024,768]{1,0:T(8,128)(2,1)} %get-tuple-element.102.refs_2_.refs_1_, f32[1024,768]{1,0:T(8,128)} %get-tuple-element.125.refs_2_, ...), custom_call_target="tpu_custom_call" | custom-call | flops 3623878656 | bytes 9879552 | tf_op jit(solution)/shard_map/input_back/pallas_call | solution.py:88
  192.8 1.6 pack.1
  194.4 8.5 %collective-permute-done.16.refs_3_.refs_4_ = bf16[1152,384]{1,0:T(8,128)(2,1)S(1)} collective-permute-done((bf16[1152,384]{1,0:T(8,128)(2,1)}, bf16[1152,384]{1,0:T(8,128)(2,1)S(1)}, u32[]{:S(2)}, u32[]{:S(2)}) %collective-permute-start.16) | collective-permute-done | bytes 884768 | tf_op jit(solution)/shard_map/ppermute | solution.py:871
  202.9 1.5 collective-permute-done.17.refs_7_.refs_8_
  204.4 0.9 copy-done.2
  205.3 4.4 %halve.1 = (bf16[576,384]{1,0:T(8,128)(2,1)}, bf16[576,384]{1,0:T(8,128)(2,1)}, bf16[576,384]{1,0:T(8,128)(2,1)}, bf16[576,384]{1,0:T(8,128)(2,1)}) custom-call(s32[7]{0:T(128)} %stack.63.refs_0_, bf16[1152,384]{1,0:T(8,128)(2,1)} %get-tuple-element.145.refs_1_.refs_2_, bf16[1152,384]{1,0:T(8,128)(2,1)} %get-tuple-element.145.refs_1_.refs_2_, ...), custom_call_target="tpu_custom_call" | custom-call | bytes 3538944 | tf_op jit(solution)/shard_map/halve/pallas_call | solution.py:88
  209.7 1.6 collective-permute-start.21
  211.9 1.4 collective-permute-done.19.refs_3_
  213.3 0.7 copy-done.21
  214.3 3.7 %tokens_place.1 = (bf16[2,512,768]{2,1,0:T(8,128)(2,1)}, f32[2,512,768]{2,1,0:T(8,128)}, f32[2,128,768]{2,1,0:T(8,128)}) custom-call(s32[7]{0:T(128)} %stack.63.refs_0_, bf16[512,768]{1,0:T(8,128)(2,1)} %copy-done.8, bf16[512,768]{1,0:T(8,128)(2,1)} %copy-done.9, ...), custom_call_target="tpu_custom_call", output_to_operand_aliasing={{0}: (4, {}), {1}: (5, {}), {2}: (6, {})} | custom-call | bytes 11010048 | tf_op jit(solution)/shard_map/tokens_place/pallas_call | solution.py:88
  218.0 7.0 %collective-permute-done.21.refs_2_ = bf16[576,384]{1,0:T(8,128)(2,1)S(1)} collective-permute-done((bf16[576,384]{1,0:T(8,128)(2,1)}, bf16[576,384]{1,0:T(8,128)(2,1)S(1)}, u32[]{:S(2)}, u32[]{:S(2)}) %collective-permute-start.21) | collective-permute-done | bytes 442400 | tf_op jit(solution)/shard_map/ppermute | solution.py:871
  225.0 0.8 copy-done.12
  225.9 3.1 share.1
  229.0 1.5 collective-permute-start.25
  230.5 2.6 collective-permute-start.26
  233.4 1.2 collective-permute-done.20.refs_1_
  235.2 1.4 small_add.5.refs_0_.refs_2_
  237.3 4.0 %collective-permute-done.23.refs_1_ = f32[96,128]{1,0:T(8,128)S(1)} collective-permute-done((f32[96,128]{1,0:T(8,128)}, f32[96,128]{1,0:T(8,128)S(1)}, u32[]{:S(2)}, u32[]{:S(2)}) %collective-permute-start.23) | collective-permute-done | bytes 49184 | tf_op jit(solution)/shard_map/ppermute | solution.py:871
  241.9 1.4 small_add.6.refs_4_.refs_0_
  243.4 8.4 %collective-permute-done.26.refs_2_ = bf16[288,384]{1,0:T(8,128)(2,1)S(1)} collective-permute-done((bf16[288,384]{1,0:T(8,128)(2,1)}, bf16[288,384]{1,0:T(8,128)(2,1)S(1)}, u32[]{:S(2)}, u32[]{:S(2)}) %collective-permute-start.26) | collective-permute-done | bytes 221216 | tf_op jit(solution)/shard_map/ppermute | solution.py:871
  251.8 0.7 copy-done.16
  252.6 2.1 total.1.refs_2_.refs_1_
  254.6 2.4 collective-permute-start.31
  257.1 6.4 %collective-permute-start.30 = (bf16[288,384]{1,0:T(8,128)(2,1)}, bf16[288,384]{1,0:T(8,128)(2,1)S(1)}, u32[]{:S(2)}, u32[]{:S(2)}) collective-permute-start(bf16[288,384]{1,0:T(8,128)(2,1)} %total.1.refs_2_.refs_1_), channel_id=1, source_target_pairs={{0,16},{2,18},{4,20},{6,22},{8,24},{10,26},{12,28},{14,30},{16,0},... | collective-permute-start | bytes 663560 | tf_op jit(solution)/shard_map/ppermute | solution.py:871
  263.5 1.3 collective-permute-start.24
  264.8 3.9 %collective-permute-done.24.refs_1_ = f32[96,128]{1,0:T(8,128)S(1)} collective-permute-done((f32[96,128]{1,0:T(8,128)}, f32[96,128]{1,0:T(8,128)S(1)}, u32[]{:S(2)}, u32[]{:S(2)}) %collective-permute-start.24) | collective-permute-done | bytes 49184 | tf_op jit(solution)/shard_map/ppermute | solution.py:871
  269.3 1.4 small_add.7.refs_5_.refs_0_
  270.8 13.1 %collective-permute-done.30.refs_3_ = bf16[288,384]{1,0:T(8,128)(2,1)S(1)} collective-permute-done((bf16[288,384]{1,0:T(8,128)(2,1)}, bf16[288,384]{1,0:T(8,128)(2,1)S(1)}, u32[]{:S(2)}, u32[]{:S(2)}) %collective-permute-start.30) | collective-permute-done | bytes 221216 | tf_op jit(solution)/shard_map/ppermute | solution.py:871
  283.9 0.7 copy-done.19
  284.5 0.7 copy-done.20
  285.2 3.0 spread.1.refs_2_.refs_1_
  288.2 1.4 collective-permute-start.35
  290.2 1.5 collective-permute-start.33
  291.7 7.6 %collective-permute-done.28.refs_1_ = f32[96,128]{1,0:T(8,128)S(1)} collective-permute-done((f32[96,128]{1,0:T(8,128)S(1)}, f32[96,128]{1,0:T(8,128)S(1)}, u32[]{:S(2)}, u32[]{:S(2)}) %collective-permute-start.28) | collective-permute-done | bytes 49184 | tf_op jit(solution)/shard_map/ppermute | solution.py:871
  299.9 1.4 small_add.8.refs_0_.refs_2_
  301.4 7.2 %collective-permute-done.32.refs_1_ = f32[96,128]{1,0:T(8,128)S(1)} collective-permute-done((f32[96,128]{1,0:T(8,128)}, f32[96,128]{1,0:T(8,128)S(1)}, u32[]{:S(2)}, u32[]{:S(2)}) %collective-permute-start.32) | collective-permute-done | bytes 49184 | tf_op jit(solution)/shard_map/ppermute | solution.py:871
  309.2 1.4 small_add.9.refs_5_
  310.6 0.7 slice.45
  311.3 0.8 slice_reduce_fusion
  313.5 1.4 slice_bitcast_fusion.1
  315.5 1.3 slice_bitcast_fusion
  316.8 3.6 %collective-permute-done.35.refs_4_ = bf16[1152,384]{1,0:T(8,128)(2,1)S(1)} collective-permute-done((bf16[1152,384]{1,0:T(8,128)(2,1)}, bf16[1152,384]{1,0:T(8,128)(2,1)S(1)}, u32[]{:S(2)}, u32[]{:S(2)}) %collective-permute-start.35) | collective-permute-done | bytes 884768 | tf_op jit(solution)/shard_map/ppermute | solution.py:871
  320.4 17.9 %collective-permute-done.34.refs_3_ = bf16[1152,384]{1,0:T(8,128)(2,1)S(1)} collective-permute-done((bf16[1152,384]{1,0:T(8,128)(2,1)}, bf16[1152,384]{1,0:T(8,128)(2,1)S(1)}, u32[]{:S(2)}, u32[]{:S(2)}) %collective-permute-start.34) | collective-permute-done | bytes 884768 | tf_op jit(solution)/shard_map/ppermute | solution.py:871
  338.3 0.9 copy-done.6
  339.2 0.9 copy-done.7
  340.2 6.2 %mixed_place.1 = (f32[2304,384]{1,0:T(8,128)}, f32[768,1536]{1,0:T(8,128)}, f32[384,768]{1,0:T(8,128)}) custom-call(s32[7]{0:T(128)} %stack.63.refs_0_, bf16[1152,384]{1,0:T(8,128)(2,1)} %spread.1.refs_2_.refs_1_, bf16[1152,384]{1,0:T(8,128)(2,1)} %copy-done.7, bf16[1152,384]{1,0:T(8,128)(2,1)} %copy-done.6, bf16[1152,384]{1,0:T(8,128)(2,1)} %copy-done.5, ...), custom_call_target="tpu_custom_call" | custom-call | bytes 18874368 | tf_op jit(solution)/shard_map/mixed_place/pallas_call | solution.py:88
  346.3 5.3 %feed_place.1 = (f32[768,1536]{1,0:T(8,128)}, f32[1536,768]{1,0:T(8,128)}) custom-call(bf16[768,768]{1,0:T(8,128)(2,1)} %get-tuple-element.207.refs_0_, bf16[1536,768]{1,0:T(8,128)(2,1)} %get-tuple-element.208.refs_1_, f32[768,1536]{1,0:T(8,128)} %get-tuple-element.170.refs_2_, f32[384,768]{1,0:T(8,128)} %get-tuple-element.199.refs_3_), custom_call_target="tpu_custom_call", output_to_operand_aliasing={{0}: (2, {})} | custom-call | bytes 18874368 | tf_op jit(solution)/shard_map/feed_place/pallas_call | solution.py:88
  (149 shorter events, 16.4 us)
Async XLA Ops:
  7.2 3.4 copy-start.37
  7.2 3.5 copy-start.36
  7.2 3.9 %copy-start.29 = (f32[768]{0:T(1024)S(1)}, f32[768]{0:T(1024)}, u32[]{:S(2)}) copy-start(f32[768]{0:T(1024)} %param.21) | copy-start | bytes 9220
  7.2 3.9 %copy-start.30 = (f32[768]{0:T(1024)S(1)}, f32[768]{0:T(1024)}, u32[]{:S(2)}) copy-start(f32[768]{0:T(1024)} %param.22) | copy-start | bytes 9220
  7.2 3.9 %copy-start.31 = (f32[768]{0:T(1024)S(1)}, f32[768]{0:T(1024)}, u32[]{:S(2)}) copy-start(f32[768]{0:T(1024)} %param.28) | copy-start | bytes 9220
  7.2 3.9 %copy-start.32 = (f32[768]{0:T(1024)S(1)}, f32[768]{0:T(1024)}, u32[]{:S(2)}) copy-start(f32[768]{0:T(1024)} %param.29) | copy-start | bytes 9220
  7.3 4.0 %copy-start.33 = (f32[768]{0:T(1024)S(1)}, f32[768]{0:T(1024)}, u32[]{:S(2)}) copy-start(f32[768]{0:T(1024)} %param.30) | copy-start | bytes 9220
  7.3 4.0 %copy-start.34 = (f32[768]{0:T(1024)S(1)}, f32[768]{0:T(1024)}, u32[]{:S(2)}) copy-start(f32[768]{0:T(1024)} %param.34) | copy-start | bytes 9220
  7.3 5.3 %copy-start.35 = (bf16[1536]{0:T(1024)(128)(2,1)S(1)}, bf16[1536]{0:T(1024)(128)(2,1)}, u32[]{:S(2)}) copy-start(bf16[1536]{0:T(1024)(128)(2,1)} %param.32) | copy-start | bytes 9220
  7.3 6.3 %copy-start.28 = (bf16[2,6,256]{2,0,1:T(2,128)(2,1)S(1)}, bf16[2,6,256]{2,0,1:T(2,128)(2,1)}, u32[]{:S(2)}) copy-start(bf16[2,6,256]{2,0,1:T(2,128)(2,1)} %param.25) | copy-start | bytes 18436
  7.3 339.0 %all-reduce.3.cloned.1.call-start = ((), (), s32[]{:S(2)}) async-start(), calls=%async_computation | async-start | bytes 7077888 | tf_op jit(solution)/shard_map/psum | solution.py:1350
  7.3 6.5 %collective-permute-start.1 = (bf16[3,768,384]{2,1,0:T(8,128)(2,1)}, bf16[3,768,384]{2,1,0:T(8,128)(2,1)S(1)}, u32[]{:S(2)}, u32[]{:S(2)}) collective-permute-start(bf16[3,768,384]{2,1,0:T(8,128)(2,1)} %bitcast.35), channel_id=1, source_target_pairs={{0,1},{1,0},{2,3},{3,2},{4,5},{5,4},{6,7},{7,6},{8,9},{9,8},{10,11... | collective-permute-start | bytes 5308424 | tf_op jit(solution)/shard_map/ppermute | solution.py:867
  9.0 4.7 %collective-permute-start = (bf16[512,768]{1,0:T(8,128)(2,1)S(1)}, bf16[512,768]{1,0:T(8,128)(2,1)}, u32[]{:S(2)}, u32[]{:S(2)}) collective-permute-start(bf16[512,768]{1,0:T(8,128)(2,1)S(1)} %dynamic-slice_bitcast_fusion.1), channel_id=1, source_target_pairs={{0,1},{1,0},{2,3},{3,2},{4,5},{5,4},{6,7},{7,6},{8,9},{9,8},{10,11... | collective-permute-start | bytes 2359304 | tf_op jit(solution)/shard_map/ppermute | solution.py:867
  10.1 3.4 collective-permute-start.3
  10.6 15.9 %collective-permute-start.5 = (bf16[2,6]{1,0:T(2,128)(2,1)S(1)}, bf16[2,6]{1,0:T(2,128)(2,1)S(1)}, u32[]{:S(2)}, u32[]{:S(2)}) collective-permute-start(bf16[2,6]{1,0:T(2,128)(2,1)S(1)} %copy-done.37), channel_id=1, source_target_pairs={{0,1},{1,0},{2,3},{3,2},{4,5},{5,4},{6,7},{7,6},{8,9},{9,8},{10,11... | collective-permute-start | bytes 80 | tf_op jit(solution)/shard_map/ppermute | solution.py:867
  10.7 1.9 collective-permute-start.2
  12.6 14.0 %collective-permute-start.6 = (bf16[1536]{0:T(1024)(128)(2,1)S(1)}, bf16[1536]{0:T(1024)(128)(2,1)S(1)}, u32[]{:S(2)}, u32[]{:S(2)}) collective-permute-start(bf16[1536]{0:T(1024)(128)(2,1)S(1)} %copy-done.35), channel_id=1, source_target_pairs={{0,1},{1,0},{2,3},{3,2},{4,5},{5,4},{6,7},{7,6},{8,9},{9,8},{10,11... | collective-permute-start | bytes 9224 | tf_op jit(solution)/shard_map/ppermute | solution.py:867
  13.5 13.0 %copy-start.38 = (bf16[768,1536]{1,0:T(8,128)(2,1)S(1)}, bf16[768,1536]{1,0:T(8,128)(2,1)}, u32[]{:S(2)}) copy-start(bf16[768,1536]{1,0:T(8,128)(2,1)} %refs_10_.1) | copy-start | bytes 7077892
  13.5 15.5 %copy-start.43 = (bf16[384,768]{1,0:T(8,128)(2,1)S(1)}, bf16[384,768]{1,0:T(8,128)(2,1)}, u32[]{:S(2)}) copy-start(bf16[384,768]{1,0:T(8,128)(2,1)} %refs_4_.1) | copy-start | bytes 1769476
  13.5 15.9 %copy-start.14 = (bf16[2,512,768]{2,1,0:T(8,128)(2,1)S(1)}, bf16[2,512,768]{2,1,0:T(8,128)(2,1)}, u32[]{:S(2)}) copy-start(bf16[2,512,768]{2,1,0:T(8,128)(2,1)} %refs_6_.1) | copy-start | bytes 4718596
  13.6 13.0 %collective-permute-start.4 = (bf16[2,6,256]{2,0,1:T(2,128)(2,1)S(1)}, bf16[2,6,256]{2,0,1:T(2,128)(2,1)S(1)}, u32[]{:S(2)}, u32[]{:S(2)}) collective-permute-start(bf16[2,6,256]{2,0,1:T(2,128)(2,1)S(1)} %copy-done.28), channel_id=1, source_target_pairs={{0,1},{1,0},{2,3},{3,2},{4,5},{5,4},{6,7},{7,6},{8,9},{9,8},{10,11... | collective-permute-start | bytes 18440 | tf_op jit(solution)/shard_map/ppermute | solution.py:867
  26.6 21.8 %collective-permute-start.9 = (bf16[768,1536]{1,0:T(8,128)(2,1)S(1)}, bf16[768,1536]{1,0:T(8,128)(2,1)S(1)}, u32[]{:S(2)}, u32[]{:S(2)}) collective-permute-start(bf16[768,1536]{1,0:T(8,128)(2,1)S(1)} %copy-done.38), channel_id=1, source_target_pairs={{0,1},{1,0},{2,3},{3,2},{4,5},{5,4},{6,7},{7,6},{8,9},{9,8},{10,11... | collective-permute-start | bytes 7077896 | tf_op jit(solution)/shard_map/ppermute | solution.py:867
  27.0 21.4 %collective-permute-start.10 = (bf16[1536,768]{1,0:T(8,128)(2,1)}, bf16[1536,768]{1,0:T(8,128)(2,1)}, u32[]{:S(2)}, u32[]{:S(2)}) collective-permute-start(bf16[1536,768]{1,0:T(8,128)(2,1)} %refs_14_.1), channel_id=1, source_target_pairs={{0,1},{1,0},{2,3},{3,2},{4,5},{5,4},{6,7},{7,6},{8,9},{9,8},{10,11... | collective-permute-start | bytes 7077896 | tf_op jit(solution)/shard_map/ppermute | solution.py:867
  29.1 19.3 %collective-permute-start.7 = (bf16[384,768]{1,0:T(8,128)(2,1)S(1)}, bf16[384,768]{1,0:T(8,128)(2,1)}, u32[]{:S(2)}, u32[]{:S(2)}) collective-permute-start(bf16[384,768]{1,0:T(8,128)(2,1)S(1)} %copy-done.43), channel_id=1, source_target_pairs={{0,1},{1,0},{2,3},{3,2},{4,5},{5,4},{6,7},{7,6},{8,9},{9,8},{10,11... | collective-permute-start | bytes 1769480 | tf_op jit(solution)/shard_map/ppermute | solution.py:867
  29.5 18.9 %collective-permute-start.8 = (bf16[512,768]{1,0:T(8,128)(2,1)S(1)}, bf16[512,768]{1,0:T(8,128)(2,1)S(1)}, u32[]{:S(2)}, u32[]{:S(2)}) collective-permute-start(bf16[512,768]{1,0:T(8,128)(2,1)S(1)} %dynamic-slice_bitcast_fusion), channel_id=1, source_target_pairs={{0,1},{1,0},{2,3},{3,2},{4,5},{5,4},{6,7},{7,6},{8,9},{9,8},{10,11... | collective-permute-start | bytes 2359304 | tf_op jit(solution)/shard_map/ppermute | solution.py:867
  48.4 1.6 copy-start.39
  115.8 23.2 %collective-permute-start.12 = (bf16[768,1536]{1,0:T(8,128)(2,1)}, bf16[768,1536]{1,0:T(8,128)(2,1)S(1)}, u32[]{:S(2)}, u32[]{:S(2)}) collective-permute-start(bf16[768,1536]{1,0:T(8,128)(2,1)} %get-tuple-element.114), channel_id=1, source_target_pairs={{0,1},{1,0},{2,3},{3,2},{4,5},{5,4},{6,7},{7,6},{8,9},{9,8},{10,11... | collective-permute-start | bytes 7077896 | tf_op jit(solution)/shard_map/ppermute | solution.py:867
  116.2 22.7 %collective-permute-start.13 = (bf16[1536,768]{1,0:T(8,128)(2,1)}, bf16[1536,768]{1,0:T(8,128)(2,1)S(1)}, u32[]{:S(2)}, u32[]{:S(2)}) collective-permute-start(bf16[1536,768]{1,0:T(8,128)(2,1)} %get-tuple-element.116), channel_id=1, source_target_pairs={{0,1},{1,0},{2,3},{3,2},{4,5},{5,4},{6,7},{7,6},{8,9},{9,8},{10,11... | collective-permute-start | bytes 7077896 | tf_op jit(solution)/shard_map/ppermute | solution.py:867
  116.4 22.4 %copy-start.44 = (bf16[768,384]{1,0:T(8,128)(2,1)S(1)}, bf16[768,384]{1,0:T(8,128)(2,1)}, u32[]{:S(2)}) copy-start(bf16[768,384]{1,0:T(8,128)(2,1)} %get-tuple-element.139) | copy-start | bytes 1769476
  138.4 29.1 %collective-permute-start.14 = (bf16[2304,384]{1,0:T(8,128)(2,1)}, bf16[2304,384]{1,0:T(8,128)(2,1)}, u32[]{:S(2)}, u32[]{:S(2)}) collective-permute-start(bf16[2304,384]{1,0:T(8,128)(2,1)} %get-tuple-element.137), channel_id=1, source_target_pairs={{0,1},{1,0},{2,3},{3,2},{4,5},{5,4},{6,7},{7,6},{8,9},{9,8},{10,11... | collective-permute-start | bytes 5308424 | tf_op jit(solution)/shard_map/ppermute | solution.py:867
  138.8 28.6 %collective-permute-start.15 = (bf16[768,384]{1,0:T(8,128)(2,1)S(1)}, bf16[768,384]{1,0:T(8,128)(2,1)S(1)}, u32[]{:S(2)}, u32[]{:S(2)}) collective-permute-start(bf16[768,384]{1,0:T(8,128)(2,1)S(1)} %copy-done.44), channel_id=1, source_target_pairs={{0,1},{1,0},{2,3},{3,2},{4,5},{5,4},{6,7},{7,6},{8,9},{9,8},{10,11... | collective-permute-start | bytes 1769480 | tf_op jit(solution)/shard_map/ppermute | solution.py:867
  139.0 1.4 copy-start
  139.0 2.2 copy-start.3
  168.3 11.2 %copy-start.40 = (bf16[512,768]{1,0:T(8,128)(2,1)S(1)}, bf16[512,768]{1,0:T(8,128)(2,1)}, u32[]{:S(2)}) copy-start(bf16[512,768]{1,0:T(8,128)(2,1)} %get-tuple-element.109) | copy-start | bytes 2359300
  175.2 27.8 %collective-permute-start.16 = (bf16[1152,384]{1,0:T(8,128)(2,1)}, bf16[1152,384]{1,0:T(8,128)(2,1)S(1)}, u32[]{:S(2)}, u32[]{:S(2)}) collective-permute-start(bf16[1152,384]{1,0:T(8,128)(2,1)} %get-tuple-element.146), channel_id=1, source_target_pairs={{0,2},{2,0},{4,6},{6,4},{8,10},{10,8},{12,14},{14,12},{16,18},{18,... | collective-permute-start | bytes 2654216 | tf_op jit(solution)/shard_map/ppermute | solution.py:871
  178.0 26.4 %collective-permute-start.17 = (bf16[1152,384]{1,0:T(8,128)(2,1)}, bf16[1152,384]{1,0:T(8,128)(2,1)S(1)}, u32[]{:S(2)}, u32[]{:S(2)}) collective-permute-start(bf16[1152,384]{1,0:T(8,128)(2,1)} %get-tuple-element.140.refs_16_), channel_id=1, source_target_pairs={{0,4},{2,6},{4,0},{6,2},{8,12},{10,14},{12,8},{14,10},{16,20},{18,... | collective-permute-start | bytes 2654216 | tf_op jit(solution)/shard_map/ppermute | solution.py:871
  179.5 32.4 %collective-permute-start.11 = (bf16[512,768]{1,0:T(8,128)(2,1)S(1)}, bf16[512,768]{1,0:T(8,128)(2,1)S(1)}, u32[]{:S(2)}, u32[]{:S(2)}) collective-permute-start(bf16[512,768]{1,0:T(8,128)(2,1)S(1)} %copy-done.40), channel_id=1, source_target_pairs={{0,1},{1,0},{2,3},{3,2},{4,5},{5,4},{6,7},{7,6},{8,9},{9,8},{10,11... | collective-permute-start | bytes 2359304 | tf_op jit(solution)/shard_map/ppermute | solution.py:867
  202.9 1.5 copy-start.1
  205.3 4.4 %copy-start.41 = (bf16[512,768]{1,0:T(8,128)(2,1)S(1)}, bf16[512,768]{1,0:T(8,128)(2,1)}, u32[]{:S(2)}) copy-start(bf16[512,768]{1,0:T(8,128)(2,1)} %get-tuple-element.149) | copy-start | bytes 2359300
  205.3 6.6 %copy-start.45 = (bf16[128,768]{1,0:T(8,128)(2,1)S(1)}, bf16[128,768]{1,0:T(8,128)(2,1)}, u32[]{:S(2)}) copy-start(bf16[128,768]{1,0:T(8,128)(2,1)} %get-tuple-element.150) | copy-start | bytes 589828
  209.7 3.6 %collective-permute-start.18 = (bf16[512,768]{1,0:T(8,128)(2,1)S(1)}, bf16[512,768]{1,0:T(8,128)(2,1)S(1)}, u32[]{:S(2)}, u32[]{:S(2)}) collective-permute-start(bf16[512,768]{1,0:T(8,128)(2,1)S(1)} %copy-done.41), channel_id=1, source_target_pairs={{0,1},{1,0},{2,3},{3,2},{4,5},{5,4},{6,7},{7,6},{8,9},{9,8},{10,11... | collective-permute-start | bytes 2359304 | tf_op jit(solution)/shard_map/ppermute | solution.py:867
  209.7 15.2 %collective-permute-start.21 = (bf16[576,384]{1,0:T(8,128)(2,1)}, bf16[576,384]{1,0:T(8,128)(2,1)S(1)}, u32[]{:S(2)}, u32[]{:S(2)}) collective-permute-start(bf16[576,384]{1,0:T(8,128)(2,1)} %get-tuple-element.160), channel_id=1, source_target_pairs={{0,4},{2,6},{4,0},{6,2},{8,12},{10,14},{12,8},{14,10},{16,20},{18,... | collective-permute-start | bytes 1327112 | tf_op jit(solution)/shard_map/ppermute | solution.py:871
  211.3 13.7 %collective-permute-start.22 = (bf16[576,384]{1,0:T(8,128)(2,1)}, bf16[576,384]{1,0:T(8,128)(2,1)S(1)}, u32[]{:S(2)}, u32[]{:S(2)}) collective-permute-start(bf16[576,384]{1,0:T(8,128)(2,1)} %get-tuple-element.154.refs_7_), channel_id=1, source_target_pairs={{0,2},{2,0},{4,6},{6,4},{8,10},{10,8},{12,14},{14,12},{16,18},{18,... | collective-permute-start | bytes 1327112 | tf_op jit(solution)/shard_map/ppermute | solution.py:871
  211.9 1.4 collective-permute-start.19
  211.9 1.4 copy-start.8
  218.0 15.4 %copy-start.22 = (f32[96,128]{1,0:T(8,128)S(1)}, f32[96,128]{1,0:T(8,128)}, u32[]{:S(2)}) copy-start(f32[96,128]{1,0:T(8,128)} %get-tuple-element.159.refs_9_) | copy-start | bytes 147460
  229.0 14.4 %collective-permute-start.25 = (bf16[288,384]{1,0:T(8,128)(2,1)}, bf16[288,384]{1,0:T(8,128)(2,1)S(1)}, u32[]{:S(2)}, u32[]{:S(2)}) collective-permute-start(bf16[288,384]{1,0:T(8,128)(2,1)} %get-tuple-element.164), channel_id=1, source_target_pairs={{0,8},{2,10},{4,12},{6,14},{8,0},{10,2},{12,4},{14,6},{16,24},{18,... | collective-permute-start | bytes 663560 | tf_op jit(solution)/shard_map/ppermute | solution.py:871
  230.5 21.3 %collective-permute-start.26 = (bf16[288,384]{1,0:T(8,128)(2,1)}, bf16[288,384]{1,0:T(8,128)(2,1)S(1)}, u32[]{:S(2)}, u32[]{:S(2)}) collective-permute-start(bf16[288,384]{1,0:T(8,128)(2,1)} %get-tuple-element.165), channel_id=1, source_target_pairs={{0,16},{2,18},{4,20},{6,22},{8,24},{10,26},{12,28},{14,30},{16,0},... | collective-permute-start | bytes 663560 | tf_op jit(solution)/shard_map/ppermute | solution.py:871
  233.1 18.7 %collective-permute-start.27 = (bf16[288,384]{1,0:T(8,128)(2,1)}, bf16[288,384]{1,0:T(8,128)(2,1)S(1)}, u32[]{:S(2)}, u32[]{:S(2)}) collective-permute-start(bf16[288,384]{1,0:T(8,128)(2,1)} %get-tuple-element.162.refs_2_), channel_id=1, source_target_pairs={{0,24},{2,26},{4,28},{6,30},{8,16},{10,18},{12,20},{14,22},{16,8},... | collective-permute-start | bytes 663560 | tf_op jit(solution)/shard_map/ppermute | solution.py:871
  233.4 1.2 collective-permute-start.20
  236.7 4.6 %collective-permute-start.23 = (f32[96,128]{1,0:T(8,128)}, f32[96,128]{1,0:T(8,128)S(1)}, u32[]{:S(2)}, u32[]{:S(2)}) collective-permute-start(f32[96,128]{1,0:T(8,128)} %small_add.5.refs_0_.refs_2_), channel_id=1, source_target_pairs={{0,2},{2,0},{4,6},{6,4},{8,10},{10,8},{12,14},{14,12},{16,18},{18,... | collective-permute-start | bytes 147464 | tf_op jit(solution)/shard_map/ppermute | solution.py:871
  243.4 8.4 %copy-start.15 = (bf16[288,384]{1,0:T(8,128)(2,1)}, bf16[288,384]{1,0:T(8,128)(2,1)S(1)}, u32[]{:S(2)}) copy-start(bf16[288,384]{1,0:T(8,128)(2,1)S(1)} %collective-permute-done.25.refs_1_) | copy-start | bytes 663556
  254.6 16.1 %collective-permute-start.31 = (bf16[288,384]{1,0:T(8,128)(2,1)}, bf16[288,384]{1,0:T(8,128)(2,1)S(1)}, u32[]{:S(2)}, u32[]{:S(2)}) collective-permute-start(bf16[288,384]{1,0:T(8,128)(2,1)} %total.1.refs_2_.refs_1_), channel_id=1, source_target_pairs={{0,24},{2,26},{4,28},{6,30},{8,16},{10,18},{12,20},{14,22},{16,8},... | collective-permute-start | bytes 663560 | tf_op jit(solution)/shard_map/ppermute | solution.py:871
  257.1 26.8 %collective-permute-start.30 = (bf16[288,384]{1,0:T(8,128)(2,1)}, bf16[288,384]{1,0:T(8,128)(2,1)S(1)}, u32[]{:S(2)}, u32[]{:S(2)}) collective-permute-start(bf16[288,384]{1,0:T(8,128)(2,1)} %total.1.refs_2_.refs_1_), channel_id=1, source_target_pairs={{0,16},{2,18},{4,20},{6,22},{8,24},{10,26},{12,28},{14,30},{16,0},... | collective-permute-start | bytes 663560 | tf_op jit(solution)/shard_map/ppermute | solution.py:871
  263.4 20.4 %collective-permute-start.29 = (bf16[288,384]{1,0:T(8,128)(2,1)}, bf16[288,384]{1,0:T(8,128)(2,1)S(1)}, u32[]{:S(2)}, u32[]{:S(2)}) collective-permute-start(bf16[288,384]{1,0:T(8,128)(2,1)} %total.1.refs_2_.refs_1_), channel_id=1, source_target_pairs={{0,8},{2,10},{4,12},{6,14},{8,0},{10,2},{12,4},{14,6},{16,24},{18,... | collective-permute-start | bytes 663560 | tf_op jit(solution)/shard_map/ppermute | solution.py:871
  263.5 5.1 %collective-permute-start.24 = (f32[96,128]{1,0:T(8,128)}, f32[96,128]{1,0:T(8,128)S(1)}, u32[]{:S(2)}, u32[]{:S(2)}) collective-permute-start(f32[96,128]{1,0:T(8,128)} %small_add.6.refs_4_.refs_0_), channel_id=1, source_target_pairs={{0,4},{2,6},{4,0},{6,2},{8,12},{10,14},{12,8},{14,10},{16,20},{18,... | collective-permute-start | bytes 147464 | tf_op jit(solution)/shard_map/ppermute | solution.py:871
  270.7 20.9 %copy-start.11 = (f32[96,128]{1,0:T(8,128)S(1)}, f32[96,128]{1,0:T(8,128)}, u32[]{:S(2)}) copy-start(f32[96,128]{1,0:T(8,128)} %small_add.7.refs_5_.refs_0_) | copy-start | bytes 147460
  270.7 13.1 %copy-start.18 = (bf16[288,384]{1,0:T(8,128)(2,1)}, bf16[288,384]{1,0:T(8,128)(2,1)S(1)}, u32[]{:S(2)}) copy-start(bf16[288,384]{1,0:T(8,128)(2,1)S(1)} %collective-permute-done.31.refs_4_) | copy-start | bytes 663556
  288.2 32.2 %collective-permute-start.35 = (bf16[1152,384]{1,0:T(8,128)(2,1)}, bf16[1152,384]{1,0:T(8,128)(2,1)S(1)}, u32[]{:S(2)}, u32[]{:S(2)}) collective-permute-start(bf16[1152,384]{1,0:T(8,128)(2,1)} %spread.1.refs_2_.refs_1_), channel_id=1, source_target_pairs={{0,6},{2,4},{4,2},{6,0},{8,14},{10,12},{12,10},{14,8},{16,22},{18,... | collective-permute-start | bytes 2654216 | tf_op jit(solution)/shard_map/ppermute | solution.py:871
  289.6 48.7 %collective-permute-start.34 = (bf16[1152,384]{1,0:T(8,128)(2,1)}, bf16[1152,384]{1,0:T(8,128)(2,1)S(1)}, u32[]{:S(2)}, u32[]{:S(2)}) collective-permute-start(bf16[1152,384]{1,0:T(8,128)(2,1)} %spread.1.refs_2_.refs_1_), channel_id=1, source_target_pairs={{0,4},{2,6},{4,0},{6,2},{8,12},{10,14},{12,8},{14,10},{16,20},{18,... | collective-permute-start | bytes 2654216 | tf_op jit(solution)/shard_map/ppermute | solution.py:871
  290.2 48.1 %collective-permute-start.33 = (bf16[1152,384]{1,0:T(8,128)(2,1)}, bf16[1152,384]{1,0:T(8,128)(2,1)S(1)}, u32[]{:S(2)}, u32[]{:S(2)}) collective-permute-start(bf16[1152,384]{1,0:T(8,128)(2,1)} %spread.1.refs_2_.refs_1_), channel_id=1, source_target_pairs={{0,2},{2,0},{4,6},{6,4},{8,10},{10,8},{12,14},{14,12},{16,18},{18,... | collective-permute-start | bytes 2654216 | tf_op jit(solution)/shard_map/ppermute | solution.py:871
  291.7 7.6 %collective-permute-start.28 = (f32[96,128]{1,0:T(8,128)S(1)}, f32[96,128]{1,0:T(8,128)S(1)}, u32[]{:S(2)}, u32[]{:S(2)}) collective-permute-start(f32[96,128]{1,0:T(8,128)S(1)} %copy-done.11), channel_id=1, source_target_pairs={{0,8},{2,10},{4,12},{6,14},{8,0},{10,2},{12,4},{14,6},{16,24},{18,... | collective-permute-start | bytes 147464 | tf_op jit(solution)/shard_map/ppermute | solution.py:871
  301.4 7.2 %collective-permute-start.32 = (f32[96,128]{1,0:T(8,128)}, f32[96,128]{1,0:T(8,128)S(1)}, u32[]{:S(2)}, u32[]{:S(2)}) collective-permute-start(f32[96,128]{1,0:T(8,128)} %small_add.8.refs_0_.refs_2_), channel_id=1, source_target_pairs={{0,16},{2,18},{4,20},{6,22},{8,24},{10,26},{12,28},{14,30},{16,0},... | collective-permute-start | bytes 147464 | tf_op jit(solution)/shard_map/ppermute | solution.py:871
  320.4 17.9 %copy-start.5 = (bf16[1152,384]{1,0:T(8,128)(2,1)}, bf16[1152,384]{1,0:T(8,128)(2,1)S(1)}, u32[]{:S(2)}) copy-start(bf16[1152,384]{1,0:T(8,128)(2,1)S(1)} %collective-permute-done.35.refs_4_) | copy-start | bytes 2654212
  (19 other events, 14.9 us)
Sparse Core Ops, SparseCore 0:
  145.8 197.4 all-reduce.2
